TPU v7x, 128 devices: a whole 4x4x4 slice. The times are simulated.
128 devices in a mesh: sec: 2 (over core), dev: 64 (over x, z, y).
Axes of the slice: x: 4, y: 4, z: 4, core: 2. Of those that a mesh axis runs over, the one named last changes fastest.
Arguments:
- hidden_in: bfloat16 [256, 7168], P(('sec', 'dev')), may hold values from -0.29882812 to 0.29882812
- queries: bfloat16 [256, 128, 576], P(('sec', 'dev')), may hold values from -40 to 40
- latent_cache: bfloat16 [256, 2048, 576], P(('sec', 'dev')), may hold values from -4.5 to 4.5
- cache_lengths: int32 [256], P(('sec', 'dev')), may hold values from 2 to 2048, as said below
- value_up: bfloat16 [128, 512, 128], P(('sec', 'dev')), may hold values from -0.25 to 0.25
- out_proj: bfloat16 [16384, 7168], P(('sec', 'dev')), may hold values from -0.046875 to 0.046875
- norm_gain: float32 [7168], replicated, may hold values from 0.5 to 1.5
- expert_ids: int32 [256, 8], P(('sec', 'dev')), may hold values from 0 to 15, all different within a row; in each aligned block of 2 rows (0 to 1, 2 to 3, ...) at most 2 rows name the same one
- route_weights: float32 [256, 8], P(('sec', 'dev')), may hold values from 0.1 to 0.5
- w_gate: bfloat16 [7168, 32768], P(None, ('sec', 'dev')), may hold values from -0.0625 to 0.0625
- w_up: bfloat16 [7168, 32768], P(None, ('sec', 'dev')), may hold values from -0.0625 to 0.0625
- w_down: bfloat16 [32768, 7168], P(('sec', 'dev')), may hold values from -0.125 to 0.125
Outputs:
- layer_out: bfloat16 [256, 7168], P(('sec', 'dev'))
Inputs may be any that keep to these rules, and one draw needn't show every extreme that they name: `expert_ids`: each row names 8 different experts, and in the rows of one device no expert is named by more than 2 rows. `cache_lengths`: some row has exactly 2048 live positions.
All inputs are finite; a program needn't handle non-finite values.
Results may differ from a plain program's by a relative error of at most 0.022.
Values may be sent and summed in bfloat16 or wider, within the bound.
A program may use at most 128 MiB of HBM per device.

v0:
```python
import jax
import jax.numpy as jnp
from jax import lax
from jax.sharding import PartitionSpec as P

EXPERTS = 16
MOST = 2


score_scale = 0.07216878364870322


def expert_pieces(slots, w_gate, w_up, w_down):
    width = slots.shape[-1]
    flat = slots.reshape(-1, width)
    gate = jnp.dot(flat, w_gate, preferred_element_type=jnp.float32)
    upper = jnp.dot(flat, w_up, preferred_element_type=jnp.float32)
    part_hidden = (jax.nn.silu(gate) * upper).astype(jnp.bfloat16)
    part_out = jnp.dot(part_hidden, w_down, preferred_element_type=jnp.float32).astype(jnp.bfloat16)
    return part_out.reshape(slots.shape)


def per_device(
    hidden_in,
    queries,
    latent_cache,
    cache_lengths,
    value_up,
    out_proj,
    norm_gain,
    expert_ids,
    route_weights,
    w_gate,
    w_up,
    w_down,
):
    rows = queries.shape[0]
    heads = queries.shape[1]
    latent = value_up.shape[1]
    span = latent_cache.shape[1]
    width = hidden_in.shape[1]
    devices = lax.axis_size(("sec", "dev"))
    block = min(512, span)

    def attend_block(index, carry):
        peak, total, summed = carry
        start = index * block
        cache = lax.dynamic_slice_in_dim(latent_cache, start, block, 1)
        score = (
            jnp.einsum("rhc,rlc->rhl", queries, cache, preferred_element_type=jnp.float32)
            * score_scale
        )
        position = start + jnp.arange(block, dtype=jnp.int32)
        live = position[None, None, :] < cache_lengths[:, None, None]
        score = jnp.where(live, score, -1e30)
        new_peak = jnp.maximum(peak, jnp.max(score, axis=-1))
        weight = jnp.where(live, jnp.exp(score - new_peak[:, :, None]), 0.0)
        factor = jnp.exp(peak - new_peak)
        total = total * factor + jnp.sum(weight, axis=-1)
        values = cache[:, :, :latent]
        summed = summed * factor[:, :, None] + jnp.einsum(
            "rhl,rlc->rhc", weight.astype(jnp.bfloat16), values, preferred_element_type=jnp.float32
        )
        return (new_peak, total, summed)

    start_carry = (
        jnp.full((rows, heads), -1e30, jnp.float32),
        jnp.zeros((rows, heads), jnp.float32),
        jnp.zeros((rows, heads, latent), jnp.float32),
    )
    block_count = span // block
    peak, total, summed = lax.fori_loop(0, block_count, attend_block, start_carry)
    attended = (summed / total[:, :, None]).astype(jnp.bfloat16)
    by_head = lax.all_to_all(attended, ("sec", "dev"), split_axis=1, concat_axis=0, tiled=True)
    head_values = jnp.einsum(
        "rhc,hcv->rhv", by_head, value_up, preferred_element_type=jnp.float32
    ).astype(jnp.bfloat16)
    flat_values = head_values.reshape(head_values.shape[0], -1)
    attn_out = lax.psum_scatter(
        jnp.dot(flat_values, out_proj, preferred_element_type=jnp.float32),
        ("sec", "dev"),
        scatter_dimension=0,
        tiled=True,
    )
    resid = hidden_in.astype(jnp.float32) + attn_out
    mean_sq = jnp.mean(resid * resid, axis=-1, keepdims=True)
    normed = (resid * lax.rsqrt(mean_sq + 1e-06) * norm_gain).astype(jnp.bfloat16)
    pieces = devices // EXPERTS
    capacity = MOST
    named = expert_ids[:, :, None] == jnp.arange(EXPERTS, dtype=jnp.int32)[None, None, :]
    member = jnp.sum(named.astype(jnp.int32), axis=1)
    gate_sum = jnp.sum(jnp.where(named, route_weights[:, :, None], 0.0), axis=1)
    rank = jnp.cumsum(member, axis=0) - member
    slot_match = (member[:, :, None] == 1) & (
        rank[:, :, None] == jnp.arange(capacity, dtype=jnp.int32)[None, None, :]
    )
    selector = slot_match.astype(jnp.float32)
    slot_weight = selector * gate_sum[:, :, None]
    packed = jnp.einsum(
        "rec,rd->ecd", selector.astype(jnp.bfloat16), normed, preferred_element_type=jnp.float32
    ).astype(jnp.bfloat16)
    outgoing = jnp.broadcast_to(packed[:, None], (EXPERTS, pieces, capacity, width)).reshape(
        devices, capacity, width
    )
    produced = expert_pieces(
        lax.all_to_all(outgoing, ("sec", "dev"), split_axis=0, concat_axis=0, tiled=True),
        w_gate,
        w_up,
        w_down,
    )
    returned = lax.all_to_all(produced, ("sec", "dev"), split_axis=0, concat_axis=0, tiled=True)
    piece_sum = jnp.sum(
        returned.reshape(EXPERTS, pieces, capacity, width).astype(jnp.float32), axis=1
    )
    expert_sum = jnp.einsum("rec,ecd->rd", slot_weight, piece_sum)
    return (resid + expert_sum).astype(jnp.bfloat16)


def solution(mesh):
    placed = (
        P(("sec", "dev"), None),
        P(("sec", "dev"), None, None),
        P(("sec", "dev"), None, None),
        P(("sec", "dev")),
        P(("sec", "dev"), None, None),
        P(("sec", "dev"), None),
        P(),
        P(("sec", "dev"), None),
        P(("sec", "dev"), None),
        P(None, ("sec", "dev")),
        P(None, ("sec", "dev")),
        P(("sec", "dev"), None),
    )
    return jax.shard_map(
        per_device, mesh=mesh, in_specs=placed, out_specs=P(("sec", "dev"), None), check_vma=False
    )
```

profile of v0, /device:TPU:0, one launch (start us, length us, event | category | flops | bytes accessed | tf_op | source)
XLA Modules:
  0.0 370.3 jit_solution(11390589856972731016)
XLA Ops:
  6.6 20.3 %while.18 = (s32[]{:T(128)}, f32[2,128]{1,0:T(2,128)S(1)}, f32[2,128]{1,0:T(2,128)S(1)}, f32[2,128,512]{2,1,0:T(8,128)S(1)}, s32[2]{0:T(128)}, /*index=5*/bf16[2...) while((s32[]{:T(128)}, f32[2,128]{1,0:T(2,128)S(1)}, ...), condition=%wide.region_3.4_spmd.clone, body=%wide.region_0.3_spmd.clone.sunk | while | flops 286788352 | bytes 5169339 | solution.py:72
  6.6 0.9 broadcast_compare_fusion.3
  7.4 2.0 fusion.57
  9.5 0.2 fusion.59
  9.7 2.0 convolution_add_fusion.2
  11.8 0.7 broadcast_compare_fusion.3
  12.5 2.0 fusion.57
  14.8 2.0 convolution_add_fusion.2
  16.8 0.7 broadcast_compare_fusion.3
  17.5 2.0 fusion.57
  19.8 2.0 convolution_add_fusion.2
  21.8 0.7 broadcast_compare_fusion.3
  22.6 2.0 fusion.57
  24.8 2.0 convolution_add_fusion.2
  27.0 0.3 copy.34
  27.2 21.4 %all_to_all.25 = bf16[2,128,512]{2,0,1:T(2,128)(2,1)S(1)} all-to-all(bf16[2,128,512]{2,0,1:T(2,128)(2,1)S(1)} %copy.34), channel_id=1, replica_groups=mesh['sec'=2,'dev'=64] {'sec','dev'}, dimensions={1} | all-to-all | bytes 524288 | tf_op jit(solution)/shard_map/all_to_all | solution.py:74
  48.8 4.3 %fusion.18 = f32[256,7168]{1,0:T(8,128)} fusion(bf16[128,7168]{1,0:T(8,128)(2,1)S(1)} %copy-done, bf16[256,512]{1,0:T(8,128)(2,1)S(1)} %reshape.86, bf16[1,512,128]{2,1,0:T(8,128)(2,1)S(1)} %copy-done.1), kind=kOutput, calls=%fused_computation.32 | convolution fusion | flops 503349248 | bytes 9568256 | tf_op jit(solution)/shard_map/dot_general | solution.py:80
  53.1 0.6 copy-done.4
  53.9 155.7 %all-reduce.3.cloned.1.call-done = f32[256,7168]{1,0:T(8,128)} async-done(((f32[256,7168]{1,0:T(8,128)}), f32[256,7168]{1,0:T(8,128)}) %all-reduce.3.cloned.1.call-update) | async-done | bytes 7340048
  209.5 1.1 multiply_reduce_fusion
  210.7 1.3 convolution_convert_fusion.1
  212.0 0.5 copy.35
  212.5 1.9 broadcast_in_dim.92
  214.4 55.0 %all_to_all.26 = bf16[128,2,7168]{2,1,0:T(2,128)(2,1)} all-to-all(bf16[128,2,7168]{2,1,0:T(2,128)(2,1)S(1)} %bitcast.34), channel_id=1, replica_groups=mesh['sec'=2,'dev'=64] {'sec','dev'}, dimensions={0} | all-to-all | bytes 7340032 | tf_op jit(solution)/shard_map/all_to_all | solution.py:106
  269.4 8.4 %reshape.89 = bf16[256,7168]{1,0:T(8,128)(2,1)} reshape(bf16[128,2,7168]{2,1,0:T(2,128)(2,1)} %all_to_all.26) | data formatting | bytes 7340032 | tf_op jit(solution)/shard_map/reshape | solution.py:15
  277.7 4.3 %fusion.38 = f32[256,256]{1,0:T(8,128)S(1)} fusion(bf16[256,7168]{1,0:T(8,128)(2,1)} %reshape.89, bf16[7168,256]{1,0:T(8,128)(2,1)} %param.23), kind=kOutput, calls=%fused_computation.62 | convolution fusion | flops 939524096 | bytes 7602176 | tf_op jit(solution)/shard_map/dot_general | solution.py:16
  282.0 10.1 %convolution_convert_fusion = bf16[256,7168]{1,0:T(8,128)(2,1)} fusion(bf16[256,7168]{1,0:T(8,128)(2,1)} %param.25, bf16[256,7168]{1,0:T(8,128)(2,1)} %reshape.89, bf16[7168,256]{1,0:T(8,128)(2,1)} %param.24, f32[256,256]{1,0:T(8,128)S(1)} %fusion.38), kind=kOutput, calls=%fused_computation.23 | convolution fusion | flops 1881276416 | bytes 14942208 | tf_op jit(solution)/shard_map/dot_general | solution.py:19
  292.1 8.1 %reshape.90 = bf16[128,2,7168]{2,1,0:T(2,128)(2,1)} reshape(bf16[256,7168]{1,0:T(8,128)(2,1)} %convolution_convert_fusion) | data formatting | bytes 7340032 | tf_op jit(solution)/shard_map/reshape | solution.py:20
  300.3 7.8 %all-to-all-start.2 = ((bf16[128,2,7168]{2,1,0:T(2,128)(2,1)}), bf16[128,2,7168]{2,1,0:T(2,128)(2,1)}, u32[]{:S(2)}, u32[]{:S(2)}) async-start(bf16[128,2,7168]{2,1,0:T(2,128)(2,1)} %reshape.90), calls=%async_computation.2 | async-start | bytes 7340032 | tf_op jit(solution)/shard_map/all_to_all | solution.py:111
  308.2 47.7 %all-to-all-done.2 = bf16[128,2,7168]{2,1,0:T(2,128)(2,1)} async-done(((bf16[128,2,7168]{2,1,0:T(2,128)(2,1)}), bf16[128,2,7168]{2,1,0:T(2,128)(2,1)}, u32[]{:S(2)}, u32[]{:S(2)}) %all-to-all-start.2) | async-done | bytes 3670048 | tf_op jit(solution)/shard_map/all_to_all | solution.py:111
  355.9 5.7 %convert_reduce_fusion = bf16[16,2,7168]{2,1,0:T(2,128)(2,1)S(1)} fusion(bf16[128,2,7168]{2,1,0:T(2,128)(2,1)} %all-to-all-done.2), kind=kLoop, calls=%fused_computation.28 | loop fusion | flops 3440640 | bytes 4128768 | tf_op jit(solution)/shard_map/reduce_sum | solution.py:112
  361.7 1.8 fusion.16
  (43 shorter events, 1.2 us)
Async XLA Ops:
  6.5 42.2 %copy-start = (bf16[128,7168]{1,0:T(8,128)(2,1)S(1)}, bf16[128,7168]{1,0:T(8,128)(2,1)}, u32[]{:S(2)}) copy-start(bf16[128,7168]{1,0:T(8,128)(2,1)} %param.19) | copy-start | bytes 5505028
  6.5 203.0 %all-reduce.3.cloned.1.call-start = ((), (), s32[]{:S(2)}) async-start(), calls=%async_computation.3 | async-start | bytes 14680064
  6.5 42.2 %copy-start.1 = (bf16[1,512,128]{2,1,0:T(8,128)(2,1)S(1)}, bf16[1,512,128]{2,1,0:T(8,128)(2,1)}, u32[]{:S(2)}) copy-start(bf16[1,512,128]{2,1,0:T(8,128)(2,1)} %param.18) | copy-start | bytes 393220
  53.1 0.7 copy-start.4
  53.1 156.5 %copy-start.2 = (bf16[2,7168]{1,0:T(2,128)(2,1)S(1)}, bf16[2,7168]{1,0:T(2,128)(2,1)}, u32[]{:S(2)}) copy-start(bf16[2,7168]{1,0:T(2,128)(2,1)} %param.14) | copy-start | bytes 86020
  53.1 157.6 %copy-start.3 = (f32[7168]{0:T(1024)S(1)}, f32[7168]{0:T(1024)}, u32[]{:S(2)}) copy-start(f32[7168]{0:T(1024)} %param.20) | copy-start | bytes 86020
  300.3 7.8 %copy-start.5 = (f32[2,8]{1,0:T(2,128)S(1)}, f32[2,8]{1,0:T(2,128)}, u32[]{:S(2)}) copy-start(f32[2,8]{1,0:T(2,128)} %param.22) | copy-start | bytes 196
  300.3 55.7 %all-to-all-start.2 = ((bf16[128,2,7168]{2,1,0:T(2,128)(2,1)}), bf16[128,2,7168]{2,1,0:T(2,128)(2,1)}, u32[]{:S(2)}, u32[]{:S(2)}) async-start(bf16[128,2,7168]{2,1,0:T(2,128)(2,1)} %reshape.90), calls=%async_computation.2 | async-start | bytes 7340032 | tf_op jit(solution)/shard_map/all_to_all | solution.py:111
Sparse Core Ops, SparseCore 0:
  53.2 156.2 all-reduce.2
where the time goes:
time: 373 us; the launch traced here: 370 us
  waiting for transfers between devices  203 us (54%)
  blocking collectives  76.4 us (20%)
  matrix products  37.8 us (10%)
  local copies, waits for them, and re-layouts  19.9 us (5%)
  between operations  13.5 us (4%)
  other arithmetic  11.2 us (3%)
  starting transfers between devices  7.83 us (2%)
    unnamed x2, waiting for transfers between devices  156 us
    all_to_all x1, blocking collectives, per_device(): lax.all_to_all(outgoing, ('sec', 'dev'), split_axis=0, concat_axis=0, til...  55 us
    all_to_all x1, waiting for transfers between devices, per_device(): lax.all_to_all(produced, ('sec', 'dev'), split_axis=0, concat_axis=0, til...  47.7 us
    all_to_all x1, blocking collectives, per_device(): lax.all_to_all(attended, ('sec', 'dev'), split_axis=1, concat_axis=0, til...  21.4 us
    dot_general x1, matrix products, expert_pieces(): jnp.dot(part_hidden, w_down, preferred_element_type=jnp.float32)  10.1 us
    reshape x1, local copies, waits for them, and re-layouts, expert_pieces(): flat = slots.reshape(-1, width)  8.39 us
    dot_general x4, matrix products, attend_block(): jnp.einsum('rhc,rlc->rhl', queries, cache, preferred_element_type=jnp.flo...  8.12 us
    reshape x1, local copies, waits for them, and re-layouts, expert_pieces(): return part_out.reshape(slots.shape)  8.12 us
  transfers between devices with their start and end apart: 2, of which 2 were waited for; matrix products, arithmetic and copies ran while one was open for 0% of the time, Pallas kernels for 0%

commit v1 on v0

v1 whole, which is shorter than its diff:
```python
import jax
import jax.numpy as jnp
from jax import lax
from jax.experimental import pallas as pl
from jax.experimental.pallas import tpu as pltpu
from jax.sharding import PartitionSpec as P

EXPERTS = 16
ROWS_DEV = 2
MESH = pl.DeviceIdType.MESH
F32 = jnp.float32
BF16 = jnp.bfloat16
MIB = 2**20

score_scale = 0.07216878364870322

TILES = (19, 19, 18)
WIDE = 19 * 128
STARTS = (0, 2432, 4864)
WIDTHS = (2432, 2432, 2304)
SUB = 24


def dev_of(part, g, o):
    if part == 0:
        return g * 16 + o
    if part == 1:
        return (o // 4) * 16 + g * 4 + o % 4
    return o * 4 + g


def place_of(part, dev):
    if part == 0:
        return dev // 16, dev % 16
    if part == 1:
        return (dev // 4) % 4, (dev // 16) * 4 + dev % 4
    return dev % 4, dev // 4


def attend_kernel(lengths_ref, queries_ref, cache_ref, out_ref, score_ref, weight_ref, spread_ref):
    row = pl.program_id(0)
    length = lengths_ref[row]
    span = cache_ref.shape[1]
    block = 512
    query = queries_ref[0]
    peak = jnp.full((128, 1), -1e30, F32)
    for start in range(0, span, block):
        score = lax.dot_general(
            query,
            cache_ref[0, start : start + block, :],
            (((1,), (1,)), ((), ())),
            preferred_element_type=F32,
        )
        position = start + lax.broadcasted_iota(jnp.int32, (1, block), 1)
        score = jnp.where(position < length, score * score_scale, -1e30)
        score_ref[:, start : start + block] = score
        peak = jnp.maximum(peak, jnp.max(score, axis=1, keepdims=True))
    total = jnp.zeros((128, 1), F32)
    for start in range(0, span, block):
        weight = jnp.exp(score_ref[:, start : start + block] - peak)
        total = total + jnp.sum(weight, axis=1, keepdims=True)
        weight_ref[:, start : start + block] = weight.astype(BF16)
    summed = jnp.dot(weight_ref[...], cache_ref[0, :, 0:512], preferred_element_type=F32)
    attended = summed / total
    for half in range(2):
        for chunk in range(4):
            spread_ref[pl.ds(half * 4 + chunk, 64, stride=8), :] = attended[
                half * 64 : half * 64 + 64, chunk * 128 : chunk * 128 + 128
            ]
    out_ref[0] = spread_ref[...].astype(BF16)


def attend(queries, latent_cache, cache_lengths):
    rows, heads, depth = queries.shape
    span = latent_cache.shape[1]
    return pl.pallas_call(
        attend_kernel,
        grid=(rows,),
        out_shape=jax.ShapeDtypeStruct((rows, 512, 128), BF16),
        in_specs=[
            pl.BlockSpec(memory_space=pltpu.SMEM),
            pl.BlockSpec((1, heads, depth), lambda r: (r, 0, 0)),
            pl.BlockSpec((1, span, depth), lambda r: (r, 0, 0)),
        ],
        out_specs=pl.BlockSpec((1, 512, 128), lambda r: (r, 0, 0)),
        scratch_shapes=[
            pltpu.VMEM((128, span), F32),
            pltpu.VMEM((128, span), BF16),
            pltpu.VMEM((512, 128), F32),
        ],
        compiler_params=pltpu.CompilerParams(vmem_limit_bytes=40 * MIB),
        name="attend",
    )(cache_lengths, queries, latent_cache)


def key_of(part, q):
    dev = dev_of(part, q // 32, q % 16)
    return ((q // 16) % 2) * 64 + dev


def one_hot(rows_key, cols_key):
    return jnp.where(rows_key == cols_key, 1.0, 0.0).astype(BF16)


def iota(axis, shape=(128, 128)):
    return lax.broadcasted_iota(jnp.int32, shape, axis)


def layer_kernel(
    att_ref,
    hidden_ref,
    ids_ref,
    route_ref,
    gain_ref,
    value_up_ref,
    out_proj_ref,
    w_gate_ref,
    w_up_ref,
    w_down_ref,
    out_ref,
    vu_buf,
    op_buf,
    wg_buf,
    wu_buf,
    wd_buf,
    msg_buf,
    by_head,
    spread,
    heads_buf,
    sums_out,
    sums_in,
    lanes,
    plane_out,
    plane_in,
    resid_buf,
    hidden_buf,
    gain_buf,
    normed_buf,
    gather_in,
    gather_out,
    rows_in,
    rows_all,
    back_out,
    back_in,
    plane_out2,
    plane_in2,
    load_sem,
    swap_send,
    swap_recv,
    a2a_send,
    a2a_recv,
    axis_send,
    axis_recv,
    plane_send,
    plane_recv,
):
    sec = lax.axis_index("sec")
    me = lax.axis_index("dev")
    places = [place_of(part, me) for part in range(3)]

    barrier = pltpu.get_barrier_semaphore()

    def greet(step, carry):
        pl.semaphore_signal(
            barrier, inc=1, device_id=(sec, lax.rem(me + step, 64)), device_id_type=MESH
        )
        return carry

    lax.fori_loop(1, 64, greet, 0)
    pl.semaphore_signal(barrier, inc=1, device_id=(1 - sec, me), device_id_type=MESH)

    weights = (
        (value_up_ref, vu_buf),
        (out_proj_ref, op_buf),
        (w_gate_ref, wg_buf),
        (w_up_ref, wu_buf),
        (w_down_ref, wd_buf),
    )
    loads = [
        pltpu.make_async_copy(source, target.at[sec], load_sem.at[index])
        for index, (source, target) in enumerate(weights)
    ]
    swaps = [
        pltpu.make_async_remote_copy(
            source,
            target.at[sec],
            swap_send.at[index],
            swap_recv.at[index],
            device_id=(1 - sec, me),
            device_id_type=MESH,
        )
        for index, (source, target) in enumerate(weights)
    ]
    for load in loads:
        load.start()

    for index in range(64):
        msg_buf[index] = jnp.concatenate(
            [att_ref[row, index * 8 : index * 8 + 8, :].astype(F32) for row in range(ROWS_DEV)]
        ).astype(BF16)

    pl.semaphore_wait(barrier, 64)
    swaps[0].start()
    swaps[1].start()

    def send_attended(step, carry):
        peer = lax.rem(me + step, 64)
        pltpu.make_async_remote_copy(
            msg_buf.at[peer],
            by_head.at[me],
            a2a_send,
            a2a_recv,
            device_id=(sec, peer),
            device_id_type=MESH,
        ).start()
        return carry

    lax.fori_loop(1, 64, send_attended, 0)
    for swap in swaps[2:]:
        swap.start()
    by_head[me] = msg_buf[me]

    lanes[...] = jnp.zeros(lanes.shape, F32)
    hidden_buf[...] = jnp.zeros(hidden_buf.shape, F32)
    gain_buf[...] = jnp.zeros(gain_buf.shape, F32)
    hidden = hidden_ref[...].astype(F32)
    gains = gain_ref[...]
    for part in range(3):
        for tile in range(TILES[part]):
            column = STARTS[part] + tile * 128
            for row in range(ROWS_DEV):
                at = row * SUB + tile
                hidden_buf[part, at : at + 1, :] = hidden[row : row + 1, column : column + 128]
                gain_buf[part, at : at + 1, :] = gains[:, column : column + 128]

    a2a_all = pltpu.make_async_remote_copy(
        msg_buf.at[pl.ds(0, 63)],
        by_head.at[pl.ds(0, 63)],
        a2a_send,
        a2a_recv,
        device_id=(sec, lax.rem(me + 1, 64)),
        device_id_type=MESH,
    )
    loads[0].wait()
    loads[1].wait()
    swaps[0].wait_recv()
    swaps[1].wait_recv()
    a2a_all.wait_recv()

    spread[...] = by_head[...].reshape(1024, 128).astype(F32)
    for half in range(2):
        parts = []
        for row in range(ROWS_DEV):
            parts.append(
                jnp.concatenate(
                    [
                        spread[pl.ds(row * 8 + half * 4 + chunk, 64, stride=16), :].astype(BF16)
                        for chunk in range(4)
                    ],
                    axis=1,
                )
            )
        heads_buf[:, half * 128 : half * 128 + 128] = jnp.dot(
            jnp.concatenate(parts), vu_buf[half], preferred_element_type=F32
        ).astype(BF16)

    def start_axis(part, source, target, phase):
        g, o = places[part]
        for step in (1, 3, 2):
            to = lax.rem(g + step, 4)
            pltpu.make_async_remote_copy(
                source.at[part, to],
                target.at[part, g],
                axis_send.at[phase, part],
                axis_recv.at[phase, part],
                device_id=(sec, dev_of(part, to, o)),
                device_id_type=MESH,
            ).start()

    def axis_all(part, source, target, phase):
        g, o = places[part]
        return pltpu.make_async_remote_copy(
            source.at[part, pl.ds(0, 3)],
            target.at[part, pl.ds(0, 3)],
            axis_send.at[phase, part],
            axis_recv.at[phase, part],
            device_id=(sec, dev_of(part, lax.rem(g + 1, 4), o)),
            device_id_type=MESH,
        )

    def start_plane(part, source_of, target, phase):
        g, o = places[part]

        def send(step, carry):
            to = lax.rem(o + step, 16)
            pltpu.make_async_remote_copy(
                source_of(to),
                target.at[part, o],
                plane_send.at[phase, part],
                plane_recv.at[phase, part],
                device_id=(sec, dev_of(part, g, to)),
                device_id_type=MESH,
            ).start()
            return carry

        lax.fori_loop(1, 16, send, 0)

    def plane_all(part, target, phase):
        g, o = places[part]
        whole = target.at[part, pl.ds(0, 15)]
        return pltpu.make_async_remote_copy(
            whole,
            whole,
            plane_send.at[phase, part],
            plane_recv.at[phase, part],
            device_id=(sec, dev_of(part, g, lax.rem(o + 1, 16))),
            device_id_type=MESH,
        )

    def reduce_axis(part, incoming, outgoing, phase, plane_phase, target):
        g, o = places[part]
        axis_all(part, outgoing, incoming, phase).wait_recv()
        for tile in range(TILES[part]):
            columns = slice(tile * 128, tile * 128 + 128)
            total = incoming[part, 0, :, columns].astype(F32)
            for slot in range(1, 4):
                total = total + incoming[part, slot, :, columns].astype(F32)
            for row in range(ROWS_DEV):
                lanes[part, pl.ds(row * SUB + tile, 16, stride=2 * SUB), :] = total[
                    row * 16 : row * 16 + 16
                ]
        buf = plane_out if plane_phase == 0 else plane_out2
        buf[part] = lanes[part].reshape(16, 2 * SUB, 128).astype(BF16)
        target[part, o] = buf[part, o]
        start_plane(part, lambda to: buf.at[part, to], target, plane_phase)

    def reduce_plane(part, target, plane_phase):
        plane_all(part, target, plane_phase).wait_recv()
        return jnp.sum(target[part].astype(F32), axis=0)

    rows_i, cols_i = iota(0), iota(1)
    for part in range(3):
        g, o = places[part]
        ordered = jnp.dot(
            one_hot(key_of(part, rows_i), cols_i), heads_buf[...], preferred_element_type=F32
        ).astype(BF16)
        columns = slice(STARTS[part], STARTS[part] + WIDTHS[part])
        product = jnp.dot(
            ordered[:, 0:128], op_buf[0, :, columns], preferred_element_type=F32
        ) + jnp.dot(ordered[:, 128:256], op_buf[1, :, columns], preferred_element_type=F32)
        sums_out[part, :, :, 0 : WIDTHS[part]] = product.astype(BF16).reshape(4, 32, WIDTHS[part])
        if WIDTHS[part] < WIDE:
            sums_out[part, :, :, WIDTHS[part] :] = jnp.zeros((4, 32, WIDE - WIDTHS[part]), BF16)
        start_axis(part, sums_out, sums_in, 0)
        sums_in[part, g] = sums_out[part, g]
    for part in range(3):
        reduce_axis(part, sums_in, sums_out, 0, 0, plane_in)
    square = [jnp.zeros((1, 1), F32) for row in range(ROWS_DEV)]
    for part in range(3):
        resid = hidden_buf[part] + reduce_plane(part, plane_in, 0)
        resid_buf[part] = resid
        for row in range(ROWS_DEV):
            piece = resid[row * SUB : row * SUB + SUB]
            square[row] = square[row] + jnp.sum(piece * piece, keepdims=True)

    lane = iota(1, (1, 128))
    routes = []
    for row in range(ROWS_DEV):
        dense = jnp.zeros((1, 128), F32)
        for slot in range(8):
            dense = dense + jnp.where(
                lane % EXPERTS == ids_ref[row, slot], route_ref[row, slot], 0.0
            )
        high = dense.astype(BF16).astype(F32)
        middle = (dense - high).astype(BF16).astype(F32)
        low = dense - high - middle
        routes.append(
            jnp.where(
                lane < 16,
                high,
                jnp.where(lane < 32, middle, jnp.where(lane < 48, low, 0.0)),
            )
        )
    for part in range(3):
        g, o = places[part]
        for row in range(ROWS_DEV):
            block = slice(row * SUB, row * SUB + SUB)
            scale = lax.rsqrt(square[row] / 7168.0 + 1e-06)
            normed_buf[part, block, :] = resid_buf[part, block, :] * scale * gain_buf[part, block, :]
            if part == 2:
                at = row * SUB + 18
                normed_buf[part, at : at + 1, :] = routes[row]
        gather_out[part] = normed_buf[part].astype(BF16)
        gather_in[part, o] = gather_out[part]
        start_plane(part, lambda to: gather_out.at[part], gather_in, 1)
    for part in range(3):
        g, o = places[part]
        plane_all(part, gather_in, 1).wait_recv()
        lanes[part] = gather_in[part].reshape(16 * 2 * SUB, 128).astype(F32)
        for tile in range(19):
            for row in range(ROWS_DEV):
                rows_in[part, g, row * 16 : row * 16 + 16, tile * 128 : tile * 128 + 128] = lanes[
                    part, pl.ds(row * SUB + tile, 16, stride=2 * SUB), :
                ].astype(BF16)
        for step in (1, 3, 2):
            to = lax.rem(g + step, 4)
            pltpu.make_async_remote_copy(
                rows_in.at[part, g],
                rows_in.at[part, g],
                axis_send.at[1, part],
                axis_recv.at[1, part],
                device_id=(sec, dev_of(part, to, o)),
                device_id_type=MESH,
            ).start()

    for index in range(2, 5):
        loads[index].wait()
        swaps[index].wait_recv()
    gate = [jnp.zeros((128, 256), F32) for piece in range(2)]
    upper = [jnp.zeros((128, 256), F32) for piece in range(2)]
    for part in range(3):
        axis_all(part, rows_in, rows_in, 1).wait_recv()
        block = rows_in[part].reshape(128, WIDE)
        if part > 0:
            block = jnp.dot(
                one_hot(key_of(0, rows_i), key_of(part, cols_i)), block, preferred_element_type=F32
            ).astype(BF16)
        if part == 2:
            named = block[:, 2304:2432]
            block = block[:, 0:2304]
        depth = slice(STARTS[part], STARTS[part] + WIDTHS[part])
        for piece in range(2):
            gate[piece] = gate[piece] + jnp.dot(
                block, wg_buf[piece, depth, :], preferred_element_type=F32
            )
            upper[piece] = upper[piece] + jnp.dot(
                block, wu_buf[piece, depth, :], preferred_element_type=F32
            )
    rows_all[:, 512:640] = named
    for piece in range(2):
        value = gate[piece]
        rows_all[:, piece * 256 : piece * 256 + 256] = (
            value / (1.0 + jnp.exp(-value)) * upper[piece]
        ).astype(BF16)
    expert_lane = iota(1)
    for part in range(3):
        g, o = places[part]
        if part == 0:
            hidden_units = rows_all[...]
        else:
            hidden_units = jnp.dot(
                one_hot(key_of(part, rows_i), key_of(0, cols_i)),
                rows_all[...],
                preferred_element_type=F32,
            ).astype(BF16)
        columns = slice(STARTS[part], STARTS[part] + WIDTHS[part])
        product = jnp.zeros((128, WIDTHS[part]), F32)
        for piece in range(2):
            expert = piece * 8 + me // 8
            mine = (expert_lane < 48) & (expert_lane % EXPERTS == expert)
            weight = jnp.sum(
                jnp.where(mine, hidden_units[:, 512:640].astype(F32), 0.0), axis=1, keepdims=True
            )
            product = product + weight * jnp.dot(
                hidden_units[:, piece * 256 : piece * 256 + 256],
                wd_buf[piece, :, columns],
                preferred_element_type=F32,
            )
        back_out[part, :, :, 0 : WIDTHS[part]] = product.astype(BF16).reshape(4, 32, WIDTHS[part])
        if WIDTHS[part] < WIDE:
            back_out[part, :, :, WIDTHS[part] :] = jnp.zeros((4, 32, WIDE - WIDTHS[part]), BF16)
        start_axis(part, back_out, back_in, 2)
        back_in[part, g] = back_out[part, g]
    for part in range(3):
        if part == 2:
            lanes[2] = jnp.zeros(lanes.shape[1:], F32)
        reduce_axis(part, back_in, back_out, 2, 2, plane_in2)
    for part in range(3):
        resid_buf[part] = resid_buf[part] + reduce_plane(part, plane_in2, 2)
        for tile in range(TILES[part]):
            column = STARTS[part] + tile * 128
            for row in range(ROWS_DEV):
                at = row * SUB + tile
                out_ref[row : row + 1, column : column + 128] = resid_buf[part, at : at + 1, :].astype(
                    BF16
                )

    for swap in swaps:
        swap.wait_send()
    a2a_all.wait_send()
    for part in range(3):
        axis_all(part, sums_out, sums_in, 0).wait_send()
        axis_all(part, rows_in, rows_in, 1).wait_send()
        axis_all(part, back_out, back_in, 2).wait_send()
        for phase, target in enumerate((plane_in, gather_in, plane_in2)):
            plane_all(part, target, phase).wait_send()


def layer(att, hidden_in, expert_ids, route_weights, norm_gain, value_up, out_proj, w_gate, w_up, w_down):
    vmem = pl.BlockSpec(memory_space=pltpu.VMEM)
    smem = pl.BlockSpec(memory_space=pltpu.SMEM)
    hbm = pl.BlockSpec(memory_space=pl.ANY)
    dma = pltpu.SemaphoreType.DMA
    return pl.pallas_call(
        layer_kernel,
        out_shape=jax.ShapeDtypeStruct((2, 7168), BF16),
        in_specs=[vmem, vmem, smem, smem, vmem, hbm, hbm, hbm, hbm, hbm],
        out_specs=vmem,
        scratch_shapes=[
            pltpu.VMEM((2, 512, 128), BF16),
            pltpu.VMEM((2, 128, 7168), BF16),
            pltpu.VMEM((2, 7168, 256), BF16),
            pltpu.VMEM((2, 7168, 256), BF16),
            pltpu.VMEM((2, 256, 7168), BF16),
            pltpu.VMEM((64, 16, 128), BF16),
            pltpu.VMEM((64, 16, 128), BF16),
            pltpu.VMEM((1024, 128), F32),
            pltpu.VMEM((128, 256), BF16),
            pltpu.VMEM((3, 4, 32, WIDE), BF16),
            pltpu.VMEM((3, 4, 32, WIDE), BF16),
            pltpu.VMEM((3, 16 * 2 * SUB, 128), F32),
            pltpu.VMEM((3, 16, 2 * SUB, 128), BF16),
            pltpu.VMEM((3, 16, 2 * SUB, 128), BF16),
            pltpu.VMEM((3, 2 * SUB, 128), F32),
            pltpu.VMEM((3, 2 * SUB, 128), F32),
            pltpu.VMEM((3, 2 * SUB, 128), F32),
            pltpu.VMEM((3, 2 * SUB, 128), F32),
            pltpu.VMEM((3, 16, 2 * SUB, 128), BF16),
            pltpu.VMEM((3, 2 * SUB, 128), BF16),
            pltpu.VMEM((3, 4, 32, WIDE), BF16),
            pltpu.VMEM((128, 640), BF16),
            pltpu.VMEM((3, 4, 32, WIDE), BF16),
            pltpu.VMEM((3, 4, 32, WIDE), BF16),
            pltpu.VMEM((3, 16, 2 * SUB, 128), BF16),
            pltpu.VMEM((3, 16, 2 * SUB, 128), BF16),
            dma((5,)),
            dma((5,)),
            dma((5,)),
            dma,
            dma,
            dma((3, 3)),
            dma((3, 3)),
            dma((3, 3)),
            dma((3, 3)),
        ],
        compiler_params=pltpu.CompilerParams(
            collective_id=0, has_side_effects=True, vmem_limit_bytes=58 * MIB
        ),
        name="layer",
    )(
        att,
        hidden_in,
        expert_ids,
        route_weights,
        norm_gain.reshape(1, -1),
        value_up.reshape(512, 128),
        out_proj,
        w_gate,
        w_up,
        w_down,
    )


def per_device(
    hidden_in,
    queries,
    latent_cache,
    cache_lengths,
    value_up,
    out_proj,
    norm_gain,
    expert_ids,
    route_weights,
    w_gate,
    w_up,
    w_down,
):
    att = attend(queries, latent_cache, cache_lengths)
    return layer(
        att, hidden_in, expert_ids, route_weights, norm_gain, value_up, out_proj, w_gate, w_up, w_down
    )


def solution(mesh):
    rows = P(("sec", "dev"), None)
    rows3 = P(("sec", "dev"), None, None)
    placed = (
        rows,
        rows3,
        rows3,
        P(("sec", "dev")),
        rows3,
        rows,
        P(),
        rows,
        rows,
        P(None, ("sec", "dev")),
        P(None, ("sec", "dev")),
        rows,
    )
    return jax.shard_map(
        per_device, mesh=mesh, in_specs=placed, out_specs=rows, check_vma=False
    )
```

time: 373 us -> 88.2 us (0.24)
  waiting for transfers between devices: 203 us -> 0 us
  blocking collectives: 76.4 us -> 0 us
  Pallas kernels: 0 us -> 74.3 us
  matrix products: 37.8 us -> 0 us
  between operations: 13.5 us -> 0.04 us
  other arithmetic: 11.2 us -> 0 us
  starting transfers between devices: 7.83 us -> 0 us
  local copies, waits for them, and re-layouts: 19.9 us -> 13.4 us
    unnamed x2 -> x0, waiting for transfers between devices: 156 us -> none
    all_to_all x2 -> x0, blocking collectives: 76.4 us -> none  [the longest x1 55 us: per_device(): lax.all_to_all(outgoing, ('sec', 'dev'), split_axis=0, concat_axis=0, til...]
    pallas_call x0 -> x2, Pallas kernels: none -> 74.3 us  [the longest x1 70.6 us: layer(): pl.pallas_call(layer_kernel, out_shape=jax.ShapeDtypeStruct((2, 7168), BF...]
    all_to_all x1 -> x0, waiting for transfers between devices: 47.7 us -> none  [per_device(): lax.all_to_all(produced, ('sec', 'dev'), split_axis=0, concat_axis=0, til...]
    dot_general x13 -> x0, matrix products: 37.8 us -> none  [the longest x1 10.1 us: expert_pieces(): jnp.dot(part_hidden, w_down, preferred_element_type=jnp.float32)]
    reshape x2 -> x0, local copies, waits for them, and re-layouts: 16.5 us -> none  [the longest x1 8.39 us: expert_pieces(): flat = slots.reshape(-1, width)]
    unnamed x12 -> x9, local copies, waits for them, and re-layouts: 0.66 us -> 13.4 us
    reduce_sum x8 -> x0, other arithmetic: 7.88 us -> none  [the longest x1 5.73 us: per_device(): jnp.sum(returned.reshape(EXPERTS, pieces, capacity, width).astype(jnp.flo...]
  transfers between devices with their start and end apart: 2 -> 0, of which waited for: 2 -> 0; matrix products, arithmetic and copies ran while one was open for 0% -> 0% of each run, Pallas kernels for 0% -> 0%
where the time goes in v1:
time: 88.2 us; the launch traced here: 87.8 us
  Pallas kernels  74.3 us (84%)
  local copies, waits for them, and re-layouts  13.4 us (15%)
    pallas_call x1, Pallas kernels, layer(): pl.pallas_call(layer_kernel, out_shape=jax.ShapeDtypeStruct((2, 7168), BF...  70.6 us
    unnamed x9, local copies, waits for them, and re-layouts  13.4 us
    pallas_call x1, Pallas kernels, attend(): pl.pallas_call(attend_kernel, grid=(rows,), out_shape=jax.ShapeDtypeStruc...  3.66 us

profile of v1, /device:TPU:0, one launch (start us, length us, event | category | flops | bytes accessed | tf_op | source)
XLA Modules:
  0.0 87.8 jit_solution(2148406363649863699)
XLA Ops:
  0.0 1.2 %copy.13.queries_ref = bf16[2,128,576]{2,1,0:T(8,128)(2,1)S(1)} copy(bf16[2,128,576]{1,2,0:T(8,128)(2,1)} %param.13) | data formatting | bytes 589824 | tf_op args[1]
  1.2 0.0 copy-start.2
  1.2 7.7 %copy.14.cache_ref = bf16[2,2048,576]{2,1,0:T(8,128)(2,1)} copy(bf16[2,2048,576]{1,2,0:T(8,128)(2,1)} %param.14) | data formatting | bytes 9437184 | tf_op args[2]
  8.9 0.0 copy-done.2
  8.9 0.0 copy-start
  8.9 2.5 %copy-done = bf16[2,2048,576]{2,1,0:T(8,128)(2,1)S(1)} copy-done((bf16[2,2048,576]{2,1,0:T(8,128)(2,1)S(1)}, bf16[2,2048,576]{2,1,0:T(8,128)(2,1)}, u32[]{:S(2)}) %copy-start) | copy-done | bytes 4718616
  11.4 3.7 %attend.1.att_ref = bf16[2,512,128]{2,1,0:T(8,128)(2,1)S(1)} custom-call(s32[2]{0:T(128)S(1)} %copy-done.2, bf16[2,128,576]{2,1,0:T(8,128)(2,1)S(1)} %copy.13.queries_ref, bf16[2,2048,576]{2,1,0:T(8,128)(2,1)S(1)} %copy-done), custom_call_target="tpu_custom_call" | custom-call | tf_op jit(solution)/shard_map/attend/pallas_call | solution.py:76
  15.1 0.0 copy-start.1
  15.1 0.7 copy-done.1
  15.8 70.6 %layer.1 = bf16[2,7168]{1,0:T(2,128)(2,1)} custom-call(bf16[2,512,128]{2,1,0:T(8,128)(2,1)} %copy-done.1, bf16[2,7168]{1,0:T(2,128)(2,1)} %hidden_ref.1, s32[2,8]{1,0:T(2,128)} %ids_ref.1, f32[2,8]{1,0:T(2,128)} %route_ref.1, f32[1,7168]{1,0:T(1,128)} %bitcast.3, bf16[512,128]{1,0:T(8,128)(2,1)} %bitcast.2, bf16[128,7168]{1,0:T(8,128)(2,1)} %out_proj_ref.1, ...), custom_call_target="tpu_custom_call" | custom-call | tf_op jit(solution)/shard_map/layer/pallas_call | solution.py:504
  86.4 1.4 %copy.16 = bf16[2,7168]{1,0:T(2,128)(2,1)} copy(bf16[2,7168]{1,0:T(2,128)(2,1)} %layer.1) | data formatting | bytes 57344
Async XLA Ops:
  1.2 7.7 %copy-start.2 = (s32[2]{0:T(128)S(1)}, s32[2]{0:T(128)}, u32[]{:S(2)}) copy-start(s32[2]{0:T(128)} %lengths_ref.1) | copy-start | bytes 28
  8.9 2.5 %copy-start = (bf16[2,2048,576]{2,1,0:T(8,128)(2,1)S(1)}, bf16[2,2048,576]{2,1,0:T(8,128)(2,1)}, u32[]{:S(2)}) copy-start(bf16[2,2048,576]{2,1,0:T(8,128)(2,1)} %copy.14.cache_ref) | copy-start | bytes 14155780
  15.1 0.7 copy-start.1

commit v2 on v1

--- a/solution.py
+++ b/solution.py
@@ -37,62 +37,6 @@
     return dev % 4, dev // 4
 
 
-def attend_kernel(lengths_ref, queries_ref, cache_ref, out_ref, score_ref, weight_ref, spread_ref):
-    row = pl.program_id(0)
-    length = lengths_ref[row]
-    span = cache_ref.shape[1]
-    block = 512
-    query = queries_ref[0]
-    peak = jnp.full((128, 1), -1e30, F32)
-    for start in range(0, span, block):
-        score = lax.dot_general(
-            query,
-            cache_ref[0, start : start + block, :],
-            (((1,), (1,)), ((), ())),
-            preferred_element_type=F32,
-        )
-        position = start + lax.broadcasted_iota(jnp.int32, (1, block), 1)
-        score = jnp.where(position < length, score * score_scale, -1e30)
-        score_ref[:, start : start + block] = score
-        peak = jnp.maximum(peak, jnp.max(score, axis=1, keepdims=True))
-    total = jnp.zeros((128, 1), F32)
-    for start in range(0, span, block):
-        weight = jnp.exp(score_ref[:, start : start + block] - peak)
-        total = total + jnp.sum(weight, axis=1, keepdims=True)
-        weight_ref[:, start : start + block] = weight.astype(BF16)
-    summed = jnp.dot(weight_ref[...], cache_ref[0, :, 0:512], preferred_element_type=F32)
-    attended = summed / total
-    for half in range(2):
-        for chunk in range(4):
-            spread_ref[pl.ds(half * 4 + chunk, 64, stride=8), :] = attended[
-                half * 64 : half * 64 + 64, chunk * 128 : chunk * 128 + 128
-            ]
-    out_ref[0] = spread_ref[...].astype(BF16)
-
-
-def attend(queries, latent_cache, cache_lengths):
-    rows, heads, depth = queries.shape
-    span = latent_cache.shape[1]
-    return pl.pallas_call(
-        attend_kernel,
-        grid=(rows,),
-        out_shape=jax.ShapeDtypeStruct((rows, 512, 128), BF16),
-        in_specs=[
-            pl.BlockSpec(memory_space=pltpu.SMEM),
-            pl.BlockSpec((1, heads, depth), lambda r: (r, 0, 0)),
-            pl.BlockSpec((1, span, depth), lambda r: (r, 0, 0)),
-        ],
-        out_specs=pl.BlockSpec((1, 512, 128), lambda r: (r, 0, 0)),
-        scratch_shapes=[
-            pltpu.VMEM((128, span), F32),
-            pltpu.VMEM((128, span), BF16),
-            pltpu.VMEM((512, 128), F32),
-        ],
-        compiler_params=pltpu.CompilerParams(vmem_limit_bytes=40 * MIB),
-        name="attend",
-    )(cache_lengths, queries, latent_cache)
-
-
 def key_of(part, q):
     dev = dev_of(part, q // 32, q % 16)
     return ((q // 16) % 2) * 64 + dev
@@ -107,7 +51,9 @@
 
 
 def layer_kernel(
-    att_ref,
+    lengths_ref,
+    queries_ref,
+    cache_ref,
     hidden_ref,
     ids_ref,
     route_ref,
@@ -118,6 +64,9 @@
     w_up_ref,
     w_down_ref,
     out_ref,
+    cache_buf,
+    score_buf,
+    weight_buf,
     vu_buf,
     op_buf,
     wg_buf,
@@ -144,6 +93,7 @@
     back_in,
     plane_out2,
     plane_in2,
+    cache_sem,
     load_sem,
     swap_send,
     swap_recv,
@@ -166,8 +116,9 @@
         )
         return carry
 
-    lax.fori_loop(1, 64, greet, 0)
-    pl.semaphore_signal(barrier, inc=1, device_id=(1 - sec, me), device_id_type=MESH)
+    def greet_all():
+        lax.fori_loop(1, 64, greet, 0)
+        pl.semaphore_signal(barrier, inc=1, device_id=(1 - sec, me), device_id_type=MESH)
 
     weights = (
         (value_up_ref, vu_buf),
@@ -191,17 +142,59 @@
         )
         for index, (source, target) in enumerate(weights)
     ]
-    for load in loads:
-        load.start()
-
-    for index in range(64):
-        msg_buf[index] = jnp.concatenate(
-            [att_ref[row, index * 8 : index * 8 + 8, :].astype(F32) for row in range(ROWS_DEV)]
-        ).astype(BF16)
-
-    pl.semaphore_wait(barrier, 64)
-    swaps[0].start()
-    swaps[1].start()
+    span, step_len = cache_ref.shape[2], 512
+    cache_loads = [
+        [
+            pltpu.make_async_copy(
+                cache_ref.at[row, :, pl.ds(start, step_len)],
+                cache_buf.at[row, :, pl.ds(start, step_len)],
+                cache_sem.at[row, start // step_len],
+            )
+            for start in range(0, span, step_len)
+        ]
+        for row in range(ROWS_DEV)
+    ]
+    for copy in cache_loads[0] + cache_loads[1]:
+        copy.start()
+    greet_all()
+
+    for row in range(ROWS_DEV):
+        length = lengths_ref[row]
+        query = queries_ref[row].T
+        peak = jnp.full((128, 1), -1e30, F32)
+        for start in range(0, span, step_len):
+            cache_loads[row][start // step_len].wait()
+            score = jnp.dot(
+                query, cache_buf[row, :, start : start + step_len], preferred_element_type=F32
+            )
+            position = start + iota(1, (1, step_len))
+            score = jnp.where(position < length, score * score_scale, -1e30)
+            score_buf[:, start : start + step_len] = score
+            peak = jnp.maximum(peak, jnp.max(score, axis=1, keepdims=True))
+        total = jnp.zeros((128, 1), F32)
+        for start in range(0, span, step_len):
+            weight = jnp.exp(score_buf[:, start : start + step_len] - peak)
+            total = total + jnp.sum(weight, axis=1, keepdims=True)
+            weight_buf[:, start : start + step_len] = weight.astype(BF16)
+        if row == 0:
+            for load in loads:
+                load.start()
+            pl.semaphore_wait(barrier, 64)
+            swaps[0].start()
+            swaps[1].start()
+        summed = lax.dot_general(
+            weight_buf[...],
+            cache_buf[row, 0:512, :],
+            (((1,), (1,)), ((), ())),
+            preferred_element_type=F32,
+        )
+        attended = summed / total
+        for half in range(2):
+            for chunk in range(4):
+                spread[pl.ds(row * 8 + half * 4 + chunk, 64, stride=16), :] = attended[
+                    half * 64 : half * 64 + 64, chunk * 128 : chunk * 128 + 128
+                ]
+    msg_buf[...] = spread[...].astype(BF16).reshape(64, 16, 128)
 
     def send_attended(step, carry):
         peer = lax.rem(me + step, 64)
@@ -481,9 +474,7 @@
             column = STARTS[part] + tile * 128
             for row in range(ROWS_DEV):
                 at = row * SUB + tile
-                out_ref[row : row + 1, column : column + 128] = resid_buf[part, at : at + 1, :].astype(
-                    BF16
-                )
+                out_ref[row : row + 1, column : column + 128] = resid_buf[part, at : at + 1, :]
 
     for swap in swaps:
         swap.wait_send()
@@ -496,17 +487,20 @@
             plane_all(part, target, phase).wait_send()
 
 
-def layer(att, hidden_in, expert_ids, route_weights, norm_gain, value_up, out_proj, w_gate, w_up, w_down):
+def layer(lengths, queries, cache, hidden_in, expert_ids, route_weights, norm_gain, value_up, out_proj, w_gate, w_up, w_down):
     vmem = pl.BlockSpec(memory_space=pltpu.VMEM)
     smem = pl.BlockSpec(memory_space=pltpu.SMEM)
     hbm = pl.BlockSpec(memory_space=pl.ANY)
     dma = pltpu.SemaphoreType.DMA
     return pl.pallas_call(
         layer_kernel,
-        out_shape=jax.ShapeDtypeStruct((2, 7168), BF16),
-        in_specs=[vmem, vmem, smem, smem, vmem, hbm, hbm, hbm, hbm, hbm],
+        out_shape=jax.ShapeDtypeStruct((2, 7168), F32),
+        in_specs=[smem, vmem, hbm, vmem, smem, smem, vmem, hbm, hbm, hbm, hbm, hbm],
         out_specs=vmem,
         scratch_shapes=[
+            pltpu.VMEM((2, 576, 2048), BF16),
+            pltpu.VMEM((128, 2048), F32),
+            pltpu.VMEM((128, 2048), BF16),
             pltpu.VMEM((2, 512, 128), BF16),
             pltpu.VMEM((2, 128, 7168), BF16),
             pltpu.VMEM((2, 7168, 256), BF16),
@@ -533,6 +527,7 @@
             pltpu.VMEM((3, 4, 32, WIDE), BF16),
             pltpu.VMEM((3, 16, 2 * SUB, 128), BF16),
             pltpu.VMEM((3, 16, 2 * SUB, 128), BF16),
+            dma((2, 4)),
             dma((5,)),
             dma((5,)),
             dma((5,)),
@@ -548,7 +543,9 @@
         ),
         name="layer",
     )(
-        att,
+        lengths,
+        queries,
+        cache,
         hidden_in,
         expert_ids,
         route_weights,
@@ -575,10 +572,21 @@
     w_up,
     w_down,
 ):
-    att = attend(queries, latent_cache, cache_lengths)
-    return layer(
-        att, hidden_in, expert_ids, route_weights, norm_gain, value_up, out_proj, w_gate, w_up, w_down
+    out = layer(
+        cache_lengths,
+        queries.transpose(0, 2, 1),
+        latent_cache.transpose(0, 2, 1),
+        hidden_in,
+        expert_ids,
+        route_weights,
+        norm_gain,
+        value_up,
+        out_proj,
+        w_gate,
+        w_up,
+        w_down,
     )
+    return out.astype(BF16)
 
 
 def solution(mesh):

time: 88.2 us -> 75.7 us (0.86)
  local copies, waits for them, and re-layouts: 13.4 us -> 0 us
  other arithmetic: 0 us -> 1.45 us
    unnamed x9 -> x0, local copies, waits for them, and re-layouts: 13.4 us -> none
    convert_element_type x0 -> x1, other arithmetic: none -> 1.45 us  [per_device(): return out.astype(BF16)]
    pallas_call x2 -> x1, Pallas kernels: 74.3 us -> 74 us  [layer(): pl.pallas_call(layer_kernel, out_shape=jax.ShapeDtypeStruct((2, 7168), F3...]
where the time goes in v2:
time: 75.7 us; the launch traced here: 75.5 us
  Pallas kernels  74 us (98%)
  other arithmetic  1.45 us (2%)
    pallas_call x1, Pallas kernels, layer(): pl.pallas_call(layer_kernel, out_shape=jax.ShapeDtypeStruct((2, 7168), F3...  74 us

profile of v2, /device:TPU:0, one launch (start us, length us, event | category | flops | bytes accessed | tf_op | source)
XLA Modules:
  0.0 75.5 jit_solution(18401295199411457632)
XLA Ops:
  0.0 74.0 %layer.1 = f32[2,7168]{1,0:T(2,128)} custom-call(s32[2]{0:T(128)} %lengths_ref.1, bf16[2,576,128]{2,1,0:T(8,128)(2,1)} %bitcast.5, bf16[2,576,2048]{2,1,0:T(8,128)(2,1)} %bitcast.4, bf16[2,7168]{1,0:T(2,128)(2,1)} %hidden_ref.1, s32[2,8]{1,0:T(2,128)} %ids_ref.1, f32[2,8]{1,0:T(2,128)} %route_ref.1, f32[1,7168]{1,0:T(1,128)} %bitcast.7, ...), custom_call_target="tpu_custom_call" | custom-call | tf_op jit(solution)/shard_map/layer/pallas_call | solution.py:495
  74.0 1.4 %convert_element_type.3 = bf16[2,7168]{1,0:T(2,128)(2,1)} convert(f32[2,7168]{1,0:T(2,128)} %layer.1) | non-fusion elementwise | flops 14336 | bytes 86016 | tf_op jit(solution)/shard_map/convert_element_type | solution.py:589

commit v3 on v2

v3 whole, which is shorter than its diff:
```python
import jax
import jax.numpy as jnp
from jax import lax
from jax.experimental import pallas as pl
from jax.experimental.pallas import tpu as pltpu
from jax.sharding import PartitionSpec as P

EXPERTS = 16
ROWS_DEV = 2
MESH = pl.DeviceIdType.MESH
F32 = jnp.float32
BF16 = jnp.bfloat16
MIB = 2**20

score_scale = 0.07216878364870322

TILES = (11, 11, 10, 8, 8, 8, 1)
SUBS = (16, 16, 16, 8, 8, 8, 8)
FIRST = (0, 11, 22, 32, 40, 48)
CHUNKS = 6
WAVES = ((0, 1, 2), (3, 4, 5))
RING = (0, 1, 2, 1)
FAR_FIRST = sorted(
    [(x, z, y) for x in range(4) for z in range(4) for y in range(4)][1:],
    key=lambda at: -RING[at[0]] - RING[at[1]] - RING[at[2]],
)


def columns_of(chunk):
    return slice(FIRST[chunk] * 128, (FIRST[chunk] + TILES[chunk]) * 128)


class Axis:
    def __init__(self, kind):
        self.kind = kind
        self.first = (16, 4, 1)[kind]
        self.high = (4, 16, 16)[kind]
        self.low = (1, 1, 4)[kind]

    def dev(self, g, o):
        return g * self.first + (o // 4) * self.high + (o % 4) * self.low

    def place(self, dev):
        return (dev // self.first) % 4, (dev // self.high) % 4 * 4 + (dev // self.low) % 4

    def key(self, q):
        return ((q // 16) % 2) * 64 + self.dev(q // 32, q % 16)


def one_hot(rows_key, cols_key):
    return jnp.where(rows_key == cols_key, 1.0, 0.0).astype(BF16)


def iota(axis, shape=(128, 128)):
    return lax.broadcasted_iota(jnp.int32, shape, axis)


def three_terms(value):
    high = value.astype(BF16).astype(F32)
    middle = (value - high).astype(BF16).astype(F32)
    return high, middle, value - high - middle


def layer_kernel(
    lengths_ref,
    queries_ref,
    cache_ref,
    hidden_ref,
    ids_ref,
    route_ref,
    gain_ref,
    value_up_ref,
    out_proj_ref,
    w_gate_ref,
    w_up_ref,
    w_down_ref,
    out_ref,
    query_buf,
    hidden_rows,
    gain_row,
    cache_buf,
    score_buf,
    weight_buf,
    vu_buf,
    op_buf,
    wg_buf,
    wu_buf,
    wd_buf,
    msg_buf,
    by_head,
    spread,
    heads_buf,
    sums_out,
    sums_in,
    lanes,
    plane_out,
    plane_in,
    resid_buf,
    hidden_buf,
    gain_buf,
    gather_in,
    gather_out,
    rows_in,
    rows_all,
    heads_by_axis,
    units_by_axis,
    weight_by_axis,
    back_out,
    back_in,
    plane_out2,
    plane_in2,
    small_sem,
    cache_sem,
    load_sem,
    swap_send,
    swap_recv,
    a2a_send,
    a2a_recv,
    axis_send,
    axis_recv,
    plane_send,
    plane_recv,
):
    sec = lax.axis_index("sec")
    me = lax.axis_index("dev")
    axes = [Axis(kind) for kind in (0, 1, 2, 0, 1, 2, 2)]
    places = [axis.place(me) for axis in axes]

    barrier = pltpu.get_barrier_semaphore()

    def greet(step, carry):
        pl.semaphore_signal(
            barrier, inc=1, device_id=(sec, lax.rem(me + step, 64)), device_id_type=MESH
        )
        return carry

    def greet_all():
        lax.fori_loop(1, 64, greet, 0)
        pl.semaphore_signal(barrier, inc=1, device_id=(1 - sec, me), device_id_type=MESH)

    weights = (
        (value_up_ref, vu_buf),
        (out_proj_ref, op_buf),
        (w_gate_ref, wg_buf),
        (w_up_ref, wu_buf),
        (w_down_ref, wd_buf),
    )
    loads = [
        pltpu.make_async_copy(source, target.at[sec], load_sem.at[index])
        for index, (source, target) in enumerate(weights)
    ]
    swaps = [
        pltpu.make_async_remote_copy(
            source,
            target.at[sec],
            swap_send.at[index],
            swap_recv.at[index],
            device_id=(1 - sec, me),
            device_id_type=MESH,
        )
        for index, (source, target) in enumerate(weights)
    ]
    span, step_len = cache_ref.shape[2], 512
    cache_loads = [
        [
            pltpu.make_async_copy(
                cache_ref.at[row, :, pl.ds(start, step_len)],
                cache_buf.at[row, :, pl.ds(start, step_len)],
                cache_sem.at[row, start // step_len],
            )
            for start in range(0, span, step_len)
        ]
        for row in range(ROWS_DEV)
    ]
    small_loads = [
        pltpu.make_async_copy(source, target, small_sem.at[index])
        for index, (source, target) in enumerate(
            ((queries_ref, query_buf), (hidden_ref, hidden_rows), (gain_ref, gain_row))
        )
    ]
    small_loads[0].start()
    for copy in cache_loads[0] + cache_loads[1] + small_loads[1:]:
        copy.start()
    greet_all()
    small_loads[0].wait()

    for row in range(ROWS_DEV):
        length = lengths_ref[row]
        query = query_buf[row].T
        peak = jnp.full((128, 1), -1e30, F32)
        for start in range(0, span, step_len):
            cache_loads[row][start // step_len].wait()
            score = jnp.dot(
                query, cache_buf[row, :, start : start + step_len], preferred_element_type=F32
            )
            position = start + iota(1, (1, step_len))
            score = jnp.where(position < length, score * score_scale, -1e30)
            score_buf[:, start : start + step_len] = score
            peak = jnp.maximum(peak, jnp.max(score, axis=1, keepdims=True))
        total = jnp.zeros((128, 1), F32)
        for start in range(0, span, step_len):
            weight = jnp.exp(score_buf[:, start : start + step_len] - peak)
            total = total + jnp.sum(weight, axis=1, keepdims=True)
            weight_buf[:, start : start + step_len] = weight.astype(BF16)
        if row == 0:
            for load in loads:
                load.start()
            pl.semaphore_wait(barrier, 64)
            swaps[0].start()
            swaps[1].start()
        summed = lax.dot_general(
            weight_buf[...],
            cache_buf[row, 0:512, :],
            (((1,), (1,)), ((), ())),
            preferred_element_type=F32,
        )
        attended = summed / total
        for half in range(2):
            for chunk in range(4):
                spread[pl.ds(row * 8 + half * 4 + chunk, 64, stride=16), :] = attended[
                    half * 64 : half * 64 + 64, chunk * 128 : chunk * 128 + 128
                ]
    msg_buf[...] = spread[...].astype(BF16).reshape(64, 16, 128)

    for x, z, y in FAR_FIRST:
        peer = (me // 16 + x) % 4 * 16 + (me // 4 % 4 + z) % 4 * 4 + (me + y) % 4
        pltpu.make_async_remote_copy(
            msg_buf.at[peer],
            by_head.at[me],
            a2a_send,
            a2a_recv,
            device_id=(sec, peer),
            device_id_type=MESH,
        ).start()
    for swap in swaps[2:]:
        swap.start()
    by_head[me] = msg_buf[me]

    small_loads[1].wait()
    small_loads[2].wait()
    hidden = hidden_rows[...].astype(F32)
    gains = gain_row[...]
    for chunk in range(CHUNKS):
        hidden_buf[chunk][...] = jnp.zeros(hidden_buf[chunk].shape, F32)
        gain_buf[chunk][...] = jnp.zeros(gain_buf[chunk].shape, F32)
        lanes[chunk][...] = jnp.zeros(lanes[chunk].shape, F32)
        for tile in range(TILES[chunk]):
            column = (FIRST[chunk] + tile) * 128
            for row in range(ROWS_DEV):
                at = row * SUBS[chunk] + tile
                hidden_buf[chunk][at : at + 1, :] = hidden[row : row + 1, column : column + 128]
                gain_buf[chunk][at : at + 1, :] = gains[:, column : column + 128]

    a2a_all = pltpu.make_async_remote_copy(
        msg_buf.at[pl.ds(0, 63)],
        by_head.at[pl.ds(0, 63)],
        a2a_send,
        a2a_recv,
        device_id=(sec, lax.rem(me + 1, 64)),
        device_id_type=MESH,
    )
    loads[0].wait()
    loads[1].wait()
    swaps[0].wait_recv()
    swaps[1].wait_recv()
    a2a_all.wait_recv()

    spread[...] = by_head[...].reshape(1024, 128).astype(F32)
    for half in range(2):
        parts = []
        for row in range(ROWS_DEV):
            parts.append(
                jnp.concatenate(
                    [
                        spread[pl.ds(row * 8 + half * 4 + chunk, 64, stride=16), :].astype(BF16)
                        for chunk in range(4)
                    ],
                    axis=1,
                )
            )
        heads_buf[:, half * 128 : half * 128 + 128] = jnp.dot(
            jnp.concatenate(parts), vu_buf[half], preferred_element_type=F32
        ).astype(BF16)

    rows_i, cols_i = iota(0), iota(1)
    for kind in range(3):
        heads_by_axis[kind] = jnp.dot(
            one_hot(Axis(kind).key(rows_i), cols_i), heads_buf[...], preferred_element_type=F32
        ).astype(BF16)

    def axis_copy(chunk, source, target, phase, to):
        axis = axes[chunk]
        return pltpu.make_async_remote_copy(
            source,
            target,
            axis_send.at[phase, chunk],
            axis_recv.at[phase, chunk],
            device_id=(sec, axis.dev(to, places[chunk][1])),
            device_id_type=MESH,
        )

    def axis_all(chunk, target, phase):
        whole = target[chunk].at[pl.ds(0, 3)]
        return axis_copy(chunk, whole, whole, phase, lax.rem(places[chunk][0] + 1, 4))

    def start_reduce(chunk, outgoing, incoming, phase):
        g, o = places[chunk]
        for step in (2, 1, 3):
            to = lax.rem(g + step, 4)
            axis_copy(
                chunk, outgoing[chunk].at[to], incoming[chunk].at[g], phase, to
            ).start()
        incoming[chunk][g] = outgoing[chunk][g]

    def plane_copy(chunk, source, target, phase, to):
        return pltpu.make_async_remote_copy(
            source,
            target,
            plane_send.at[phase, chunk],
            plane_recv.at[phase, chunk],
            device_id=(sec, axes[chunk].dev(places[chunk][0], to)),
            device_id_type=MESH,
        )

    def plane_all(chunk, target, phase):
        whole = target[chunk].at[pl.ds(0, 15)]
        return plane_copy(chunk, whole, whole, phase, lax.rem(places[chunk][1] + 1, 16))

    def start_plane(chunk, source_of, target, phase):
        g, o = places[chunk]

        for x, high, low in FAR_FIRST:
            if x == 0:
                to = (o // 4 + high) % 4 * 4 + (o + low) % 4
                plane_copy(chunk, source_of(to), target[chunk].at[o], phase, to).start()

    def reduce_axis(chunk, incoming, outgoing, target, phase):
        g, o = places[chunk]
        axis_all(chunk, incoming, phase).wait_recv()
        sub = SUBS[chunk]
        for tile in range(TILES[chunk]):
            columns = slice(tile * 128, tile * 128 + 128)
            total = incoming[chunk][0, :, columns].astype(F32)
            for slot in range(1, 4):
                total = total + incoming[chunk][slot, :, columns].astype(F32)
            for row in range(ROWS_DEV):
                lanes[chunk][pl.ds(row * sub + tile, 16, stride=2 * sub), :] = total[
                    row * 16 : row * 16 + 16
                ]
        outgoing[chunk][...] = lanes[chunk][...].reshape(16, 2 * sub, 128).astype(BF16)
        start_plane(chunk, lambda to: outgoing[chunk].at[to], target, phase)
        target[chunk][o] = outgoing[chunk][o]

    def reduce_plane(chunk, target, phase):
        plane_all(chunk, target, phase).wait_recv()
        return jnp.sum(target[chunk][...].astype(F32), axis=0)

    def send_sums(chunk):
        heads = heads_by_axis[axes[chunk].kind]
        columns = columns_of(chunk)
        product = jnp.dot(
            heads[:, 0:128], op_buf[0, :, columns], preferred_element_type=F32
        ) + jnp.dot(heads[:, 128:256], op_buf[1, :, columns], preferred_element_type=F32)
        sums_out[chunk][...] = product.astype(BF16).reshape(sums_out[chunk].shape)
        start_reduce(chunk, sums_out, sums_in, 0)

    def add_sums(chunk):
        reduce_axis(chunk, sums_in, plane_out, plane_in, 0)

    square = [jnp.zeros((1, 1), F32) for row in range(ROWS_DEV)]

    def send_rows(chunk):
        resid = hidden_buf[chunk][...] + reduce_plane(chunk, plane_in, 0)
        resid_buf[chunk][...] = resid
        gather_out[chunk][...] = (resid * gain_buf[chunk][...]).astype(BF16)
        start_plane(chunk, lambda to: gather_out[chunk], gather_in, 1)
        gather_in[chunk][places[chunk][1]] = gather_out[chunk][...]
        for row in range(ROWS_DEV):
            piece = resid[row * SUBS[chunk] : row * SUBS[chunk] + SUBS[chunk]]
            square[row] = square[row] + jnp.sum(piece * piece, keepdims=True)

    def send_routes():
        lane = iota(1, (1, 128))
        tile_rows = iota(0, (16, 128))
        tile = jnp.zeros((16, 128), F32)
        for row in range(ROWS_DEV):
            dense = jnp.zeros((1, 128), F32)
            for slot in range(8):
                dense = dense + jnp.where(
                    lane % EXPERTS == ids_ref[row, slot], route_ref[row, slot], 0.0
                )
            factor = lax.rsqrt(square[row] / 7168.0 + 1e-06)
            dense = jnp.where(lane < 48, dense, jnp.broadcast_to(factor, (1, 128)))
            high, middle, low = three_terms(dense)
            line = jnp.where(
                (lane < 16) | (lane == 48),
                high,
                jnp.where(
                    (lane < 32) | (lane == 49),
                    middle,
                    jnp.where((lane < 48) | (lane == 50), low, 0.0),
                ),
            )
            tile = jnp.where(tile_rows == row * SUBS[CHUNKS], line, tile)
        gather_out[CHUNKS][...] = tile.astype(BF16)
        start_plane(CHUNKS, lambda to: gather_out[CHUNKS], gather_in, 1)
        gather_in[CHUNKS][places[CHUNKS][1]] = gather_out[CHUNKS][...]

    def spread_rows(chunk):
        g, o = places[chunk]
        plane_all(chunk, gather_in, 1).wait_recv()
        sub = SUBS[chunk]
        lanes[chunk][...] = gather_in[chunk][...].reshape(32 * sub, 128).astype(F32)
        for tile in range(TILES[chunk]):
            for row in range(ROWS_DEV):
                rows_in[chunk][
                    g, row * 16 : row * 16 + 16, tile * 128 : tile * 128 + 128
                ] = lanes[chunk][pl.ds(row * sub + tile, 16, stride=2 * sub), :].astype(BF16)
        for step in (2, 1, 3):
            axis_copy(
                chunk, rows_in[chunk].at[g], rows_in[chunk].at[g], 1, lax.rem(g + step, 4)
            ).start()

    gate = [jnp.zeros((128, 256), F32) for piece in range(2)]
    upper = [jnp.zeros((128, 256), F32) for piece in range(2)]

    def common_order(chunk, block):
        return jnp.dot(
            one_hot(rows_i, axes[chunk].key(cols_i)), block, preferred_element_type=F32
        ).astype(BF16)

    def expert_in(chunk):
        axis_all(chunk, rows_in, 1).wait_recv()
        block = common_order(chunk, rows_in[chunk][...].reshape(128, TILES[chunk] * 128))
        depth = columns_of(chunk)
        for piece in range(2):
            gate[piece] = gate[piece] + jnp.dot(
                block, wg_buf[piece, depth, :], preferred_element_type=F32
            )
            upper[piece] = upper[piece] + jnp.dot(
                block, wu_buf[piece, depth, :], preferred_element_type=F32
            )

    def each(step, wave):
        for chunk in WAVES[wave]:
            step(chunk)

    each(send_sums, 0)
    each(send_sums, 1)
    each(add_sums, 0)
    each(add_sums, 1)
    each(send_rows, 0)
    each(send_rows, 1)
    send_routes()
    each(spread_rows, 0)
    each(spread_rows, 1)
    spread_rows(CHUNKS)
    for index in range(2, 5):
        loads[index].wait()
        swaps[index].wait_recv()
    each(expert_in, 0)
    each(expert_in, 1)

    axis_all(CHUNKS, rows_in, 1).wait_recv()
    named = common_order(CHUNKS, rows_in[CHUNKS][...].reshape(128, 128))
    factor = jnp.sum(
        jnp.where((cols_i >= 48) & (cols_i < 51), named.astype(F32), 0.0), axis=1, keepdims=True
    )
    rows_all[:, 512:640] = named
    for piece in range(2):
        value = factor * gate[piece]
        rows_all[:, piece * 256 : piece * 256 + 256] = (
            value / (1.0 + jnp.exp(-value)) * (factor * upper[piece])
        ).astype(BF16)
    for kind in range(3):
        hidden_units = jnp.dot(
            one_hot(Axis(kind).key(rows_i), cols_i), rows_all[...], preferred_element_type=F32
        )
        units_by_axis[kind] = hidden_units[:, 0:512].astype(BF16)
        for piece in range(2):
            expert = piece * 8 + me // 8
            mine = (cols_i < 48) & (cols_i % EXPERTS == expert)
            weight = jnp.sum(
                jnp.where(mine, hidden_units[:, 512:640], 0.0), axis=1, keepdims=True
            )
            weight_by_axis[kind, piece] = jnp.broadcast_to(weight, (128, 128))

    def send_back(chunk):
        units = units_by_axis[axes[chunk].kind]
        columns = columns_of(chunk)
        product = jnp.zeros((128, TILES[chunk] * 128), F32)
        for piece in range(2):
            weight = weight_by_axis[axes[chunk].kind, piece]
            product = product + jnp.concatenate([weight] * TILES[chunk], axis=1) * jnp.dot(
                units[:, piece * 256 : piece * 256 + 256],
                wd_buf[piece, :, columns],
                preferred_element_type=F32,
            )
        back_out[chunk][...] = product.astype(BF16).reshape(back_out[chunk].shape)
        start_reduce(chunk, back_out, back_in, 2)

    def add_back(chunk):
        reduce_axis(chunk, back_in, plane_out2, plane_in2, 2)

    def finish(chunk):
        total = resid_buf[chunk][...] + reduce_plane(chunk, plane_in2, 2)
        for tile in range(TILES[chunk]):
            column = (FIRST[chunk] + tile) * 128
            for row in range(ROWS_DEV):
                at = row * SUBS[chunk] + tile
                out_ref[row : row + 1, column : column + 128] = total[at : at + 1, :]

    each(send_back, 0)
    each(send_back, 1)
    each(add_back, 0)
    each(add_back, 1)
    each(finish, 0)
    each(finish, 1)

    for swap in swaps:
        swap.wait_send()
    a2a_all.wait_send()
    for chunk in range(CHUNKS):
        axis_all(chunk, sums_in, 0).wait_send()
        axis_all(chunk, rows_in, 1).wait_send()
        axis_all(chunk, back_in, 2).wait_send()
        for phase, target in enumerate((plane_in, gather_in, plane_in2)):
            plane_all(chunk, target, phase).wait_send()
    axis_all(CHUNKS, rows_in, 1).wait_send()
    plane_all(CHUNKS, gather_in, 1).wait_send()


def layer(lengths, queries, cache, hidden_in, expert_ids, route_weights, norm_gain, value_up, out_proj, w_gate, w_up, w_down):
    vmem = pl.BlockSpec(memory_space=pltpu.VMEM)
    smem = pl.BlockSpec(memory_space=pltpu.SMEM)
    hbm = pl.BlockSpec(memory_space=pl.ANY)
    dma = pltpu.SemaphoreType.DMA
    wides = [tiles * 128 for tiles in TILES]
    return pl.pallas_call(
        layer_kernel,
        out_shape=jax.ShapeDtypeStruct((2, 7168), F32),
        in_specs=[smem, hbm, hbm, hbm, smem, smem, hbm, hbm, hbm, hbm, hbm, hbm],
        out_specs=vmem,
        scratch_shapes=[
            pltpu.VMEM((2, 576, 128), BF16),
            pltpu.VMEM((2, 7168), BF16),
            pltpu.VMEM((1, 7168), F32),
            pltpu.VMEM((2, 576, 2048), BF16),
            pltpu.VMEM((128, 2048), F32),
            pltpu.VMEM((128, 2048), BF16),
            pltpu.VMEM((2, 512, 128), BF16),
            pltpu.VMEM((2, 128, 7168), BF16),
            pltpu.VMEM((2, 7168, 256), BF16),
            pltpu.VMEM((2, 7168, 256), BF16),
            pltpu.VMEM((2, 256, 7168), BF16),
            pltpu.VMEM((64, 16, 128), BF16),
            pltpu.VMEM((64, 16, 128), BF16),
            pltpu.VMEM((1024, 128), F32),
            pltpu.VMEM((128, 256), BF16),
            [pltpu.VMEM((4, 32, wide), BF16) for wide in wides],
            [pltpu.VMEM((4, 32, wide), BF16) for wide in wides],
            [pltpu.VMEM((32 * sub, 128), F32) for sub in SUBS],
            [pltpu.VMEM((16, 2 * sub, 128), BF16) for sub in SUBS],
            [pltpu.VMEM((16, 2 * sub, 128), BF16) for sub in SUBS],
            [pltpu.VMEM((2 * sub, 128), F32) for sub in SUBS],
            [pltpu.VMEM((2 * sub, 128), F32) for sub in SUBS],
            [pltpu.VMEM((2 * sub, 128), F32) for sub in SUBS],
            [pltpu.VMEM((16, 2 * sub, 128), BF16) for sub in SUBS],
            [pltpu.VMEM((2 * sub, 128), BF16) for sub in SUBS],
            [pltpu.VMEM((4, 32, wide), BF16) for wide in wides],
            pltpu.VMEM((128, 640), BF16),
            pltpu.VMEM((3, 128, 256), BF16),
            pltpu.VMEM((3, 128, 512), BF16),
            pltpu.VMEM((3, 2, 128, 128), F32),
            [pltpu.VMEM((4, 32, wide), BF16) for wide in wides],
            [pltpu.VMEM((4, 32, wide), BF16) for wide in wides],
            [pltpu.VMEM((16, 2 * sub, 128), BF16) for sub in SUBS],
            [pltpu.VMEM((16, 2 * sub, 128), BF16) for sub in SUBS],
            dma((3,)),
            dma((2, 4)),
            dma((5,)),
            dma((5,)),
            dma((5,)),
            dma,
            dma,
            dma((3, CHUNKS + 1)),
            dma((3, CHUNKS + 1)),
            dma((3, CHUNKS + 1)),
            dma((3, CHUNKS + 1)),
        ],
        compiler_params=pltpu.CompilerParams(
            collective_id=0, has_side_effects=True, vmem_limit_bytes=58 * MIB
        ),
        name="layer",
    )(
        lengths,
        queries,
        cache,
        hidden_in,
        expert_ids,
        route_weights,
        norm_gain.reshape(1, -1),
        value_up.reshape(512, 128),
        out_proj,
        w_gate,
        w_up,
        w_down,
    )


def per_device(
    hidden_in,
    queries,
    latent_cache,
    cache_lengths,
    value_up,
    out_proj,
    norm_gain,
    expert_ids,
    route_weights,
    w_gate,
    w_up,
    w_down,
):
    out = layer(
        cache_lengths,
        queries.transpose(0, 2, 1),
        latent_cache.transpose(0, 2, 1),
        hidden_in,
        expert_ids,
        route_weights,
        norm_gain,
        value_up,
        out_proj,
        w_gate,
        w_up,
        w_down,
    )
    return out.astype(BF16)


def solution(mesh):
    rows = P(("sec", "dev"), None)
    rows3 = P(("sec", "dev"), None, None)
    placed = (
        rows,
        rows3,
        rows3,
        P(("sec", "dev")),
        rows3,
        rows,
        P(),
        rows,
        rows,
        P(None, ("sec", "dev")),
        P(None, ("sec", "dev")),
        rows,
    )
    return jax.shard_map(
        per_device, mesh=mesh, in_specs=placed, out_specs=rows, check_vma=False
    )
```

time: 75.7 us -> 65.5 us (0.87)
  Pallas kernels: 74 us -> 63.8 us
    pallas_call x1, Pallas kernels: 74 us -> 63.8 us  [layer(): pl.pallas_call(layer_kernel, out_shape=jax.ShapeDtypeStruct((2, 7168), F3...]
where the time goes in v3:
time: 65.5 us; the launch traced here: 65.3 us
  Pallas kernels  63.8 us (97%)
  other arithmetic  1.45 us (2%)
    pallas_call x1, Pallas kernels, layer(): pl.pallas_call(layer_kernel, out_shape=jax.ShapeDtypeStruct((2, 7168), F3...  63.8 us
    convert_element_type x1, other arithmetic, per_device(): return out.astype(BF16)  1.45 us

profile of v3, /device:TPU:0, one launch (start us, length us, event | category | flops | bytes accessed | tf_op | source)
XLA Modules:
  0.0 65.3 jit_solution(16799586417319953879)
XLA Ops:
  0.0 63.8 %layer.1 = f32[2,7168]{1,0:T(2,128)} custom-call(s32[2]{0:T(128)} %lengths_ref.1, bf16[2,576,128]{2,1,0:T(8,128)(2,1)} %bitcast.5, bf16[2,576,2048]{2,1,0:T(8,128)(2,1)} %bitcast.4, bf16[2,7168]{1,0:T(2,128)(2,1)} %hidden_ref.1, s32[2,8]{1,0:T(2,128)} %ids_ref.1, f32[2,8]{1,0:T(2,128)} %route_ref.1, f32[1,7168]{1,0:T(1,128)} %bitcast.7, ...), custom_call_target="tpu_custom_call" | custom-call | tf_op jit(solution)/shard_map/layer/pallas_call | solution.py:539
  63.9 1.4 %convert_element_type.3 = bf16[2,7168]{1,0:T(2,128)(2,1)} convert(f32[2,7168]{1,0:T(2,128)} %layer.1) | non-fusion elementwise | flops 14336 | bytes 86016 | tf_op jit(solution)/shard_map/convert_element_type | solution.py:639

commit v4 on v3

--- a/solution.py
+++ b/solution.py
@@ -102,6 +102,8 @@
     gather_out,
     rows_in,
     rows_all,
+    to_axis,
+    from_axis,
     heads_by_axis,
     units_by_axis,
     weight_by_axis,
@@ -128,14 +130,11 @@
 
     barrier = pltpu.get_barrier_semaphore()
 
-    def greet(step, carry):
-        pl.semaphore_signal(
-            barrier, inc=1, device_id=(sec, lax.rem(me + step, 64)), device_id_type=MESH
-        )
-        return carry
-
     def greet_all():
-        lax.fori_loop(1, 64, greet, 0)
+        for step in range(1, 64):
+            pl.semaphore_signal(
+                barrier, inc=1, device_id=(sec, lax.rem(me + step, 64)), device_id_type=MESH
+            )
         pl.semaphore_signal(barrier, inc=1, device_id=(1 - sec, me), device_id_type=MESH)
 
     weights = (
@@ -160,16 +159,8 @@
         )
         for index, (source, target) in enumerate(weights)
     ]
-    span, step_len = cache_ref.shape[2], 512
     cache_loads = [
-        [
-            pltpu.make_async_copy(
-                cache_ref.at[row, :, pl.ds(start, step_len)],
-                cache_buf.at[row, :, pl.ds(start, step_len)],
-                cache_sem.at[row, start // step_len],
-            )
-            for start in range(0, span, step_len)
-        ]
+        pltpu.make_async_copy(cache_ref.at[row], cache_buf.at[row], cache_sem.at[row])
         for row in range(ROWS_DEV)
     ]
     small_loads = [
@@ -178,48 +169,48 @@
             ((queries_ref, query_buf), (hidden_ref, hidden_rows), (gain_ref, gain_row))
         )
     ]
-    small_loads[0].start()
-    for copy in cache_loads[0] + cache_loads[1] + small_loads[1:]:
+    for copy in [small_loads[0]] + cache_loads + small_loads[1:]:
         copy.start()
     greet_all()
     small_loads[0].wait()
-
+    cache_loads[0].wait()
+    cache_loads[1].wait()
+    for load in loads:
+        load.start()
+
+    span, step_len = cache_ref.shape[2], 512
     for row in range(ROWS_DEV):
         length = lengths_ref[row]
         query = query_buf[row].T
         peak = jnp.full((128, 1), -1e30, F32)
         for start in range(0, span, step_len):
-            cache_loads[row][start // step_len].wait()
             score = jnp.dot(
                 query, cache_buf[row, :, start : start + step_len], preferred_element_type=F32
             )
             position = start + iota(1, (1, step_len))
             score = jnp.where(position < length, score * score_scale, -1e30)
-            score_buf[:, start : start + step_len] = score
+            score_buf[row, :, start : start + step_len] = score
             peak = jnp.maximum(peak, jnp.max(score, axis=1, keepdims=True))
         total = jnp.zeros((128, 1), F32)
         for start in range(0, span, step_len):
-            weight = jnp.exp(score_buf[:, start : start + step_len] - peak)
+            weight = jnp.exp(score_buf[row, :, start : start + step_len] - peak)
             total = total + jnp.sum(weight, axis=1, keepdims=True)
-            weight_buf[:, start : start + step_len] = weight.astype(BF16)
-        if row == 0:
-            for load in loads:
-                load.start()
-            pl.semaphore_wait(barrier, 64)
-            swaps[0].start()
-            swaps[1].start()
+            weight_buf[row, :, start : start + step_len] = weight.astype(BF16)
         summed = lax.dot_general(
-            weight_buf[...],
             cache_buf[row, 0:512, :],
+            weight_buf[row],
             (((1,), (1,)), ((), ())),
             preferred_element_type=F32,
         )
-        attended = summed / total
+        attended = summed.T / total
         for half in range(2):
             for chunk in range(4):
                 spread[pl.ds(row * 8 + half * 4 + chunk, 64, stride=16), :] = attended[
                     half * 64 : half * 64 + 64, chunk * 128 : chunk * 128 + 128
                 ]
+    pl.semaphore_wait(barrier, 64)
+    swaps[0].start()
+    swaps[1].start()
     msg_buf[...] = spread[...].astype(BF16).reshape(64, 16, 128)
 
     for x, z, y in FAR_FIRST:
@@ -236,6 +227,10 @@
         swap.start()
     by_head[me] = msg_buf[me]
 
+    rows_i, cols_i = iota(0), iota(1)
+    for kind in range(3):
+        to_axis[kind] = one_hot(Axis(kind).key(rows_i), cols_i)
+        from_axis[kind] = one_hot(rows_i, Axis(kind).key(cols_i))
     small_loads[1].wait()
     small_loads[2].wait()
     hidden = hidden_rows[...].astype(F32)
@@ -282,10 +277,9 @@
             jnp.concatenate(parts), vu_buf[half], preferred_element_type=F32
         ).astype(BF16)
 
-    rows_i, cols_i = iota(0), iota(1)
     for kind in range(3):
         heads_by_axis[kind] = jnp.dot(
-            one_hot(Axis(kind).key(rows_i), cols_i), heads_buf[...], preferred_element_type=F32
+            to_axis[kind], heads_buf[...], preferred_element_type=F32
         ).astype(BF16)
 
     def axis_copy(chunk, source, target, phase, to):
@@ -426,7 +420,7 @@
 
     def common_order(chunk, block):
         return jnp.dot(
-            one_hot(rows_i, axes[chunk].key(cols_i)), block, preferred_element_type=F32
+            from_axis[axes[chunk].kind], block, preferred_element_type=F32
         ).astype(BF16)
 
     def expert_in(chunk):
@@ -473,9 +467,7 @@
             value / (1.0 + jnp.exp(-value)) * (factor * upper[piece])
         ).astype(BF16)
     for kind in range(3):
-        hidden_units = jnp.dot(
-            one_hot(Axis(kind).key(rows_i), cols_i), rows_all[...], preferred_element_type=F32
-        )
+        hidden_units = jnp.dot(to_axis[kind], rows_all[...], preferred_element_type=F32)
         units_by_axis[kind] = hidden_units[:, 0:512].astype(BF16)
         for piece in range(2):
             expert = piece * 8 + me // 8
@@ -546,8 +538,8 @@
             pltpu.VMEM((2, 7168), BF16),
             pltpu.VMEM((1, 7168), F32),
             pltpu.VMEM((2, 576, 2048), BF16),
-            pltpu.VMEM((128, 2048), F32),
-            pltpu.VMEM((128, 2048), BF16),
+            pltpu.VMEM((2, 128, 2048), F32),
+            pltpu.VMEM((2, 128, 2048), BF16),
             pltpu.VMEM((2, 512, 128), BF16),
             pltpu.VMEM((2, 128, 7168), BF16),
             pltpu.VMEM((2, 7168, 256), BF16),
@@ -569,6 +561,8 @@
             [pltpu.VMEM((2 * sub, 128), BF16) for sub in SUBS],
             [pltpu.VMEM((4, 32, wide), BF16) for wide in wides],
             pltpu.VMEM((128, 640), BF16),
+            pltpu.VMEM((3, 128, 128), BF16),
+            pltpu.VMEM((3, 128, 128), BF16),
             pltpu.VMEM((3, 128, 256), BF16),
             pltpu.VMEM((3, 128, 512), BF16),
             pltpu.VMEM((3, 2, 128, 128), F32),
@@ -577,7 +571,7 @@
             [pltpu.VMEM((16, 2 * sub, 128), BF16) for sub in SUBS],
             [pltpu.VMEM((16, 2 * sub, 128), BF16) for sub in SUBS],
             dma((3,)),
-            dma((2, 4)),
+            dma((2,)),
             dma((5,)),
             dma((5,)),
             dma((5,)),

time: 65.5 us -> 64.3 us (0.982)
  Pallas kernels: 63.8 us -> 62.6 us
    pallas_call x1, Pallas kernels: 63.8 us -> 62.6 us  [layer(): pl.pallas_call(layer_kernel, out_shape=jax.ShapeDtypeStruct((2, 7168), F3...]
where the time goes in v4:
time: 64.3 us; the launch traced here: 64.1 us
  Pallas kernels  62.6 us (97%)
  other arithmetic  1.45 us (2%)
    pallas_call x1, Pallas kernels, layer(): pl.pallas_call(layer_kernel, out_shape=jax.ShapeDtypeStruct((2, 7168), F3...  62.6 us
    convert_element_type x1, other arithmetic, per_device(): return out.astype(BF16)  1.45 us

profile of v4, /device:TPU:0, one launch (start us, length us, event | category | flops | bytes accessed | tf_op | source)
XLA Modules:
  0.0 64.1 jit_solution(5215067509052961745)
XLA Ops:
  0.0 62.6 %layer.1 = f32[2,7168]{1,0:T(2,128)} custom-call(s32[2]{0:T(128)} %lengths_ref.1, bf16[2,576,128]{2,1,0:T(8,128)(2,1)} %bitcast.5, bf16[2,576,2048]{2,1,0:T(8,128)(2,1)} %bitcast.4, bf16[2,7168]{1,0:T(2,128)(2,1)} %hidden_ref.1, s32[2,8]{1,0:T(2,128)} %ids_ref.1, f32[2,8]{1,0:T(2,128)} %route_ref.1, f32[1,7168]{1,0:T(1,128)} %bitcast.7, ...), custom_call_target="tpu_custom_call" | custom-call | tf_op jit(solution)/shard_map/layer/pallas_call | solution.py:531
  62.6 1.4 %convert_element_type.3 = bf16[2,7168]{1,0:T(2,128)(2,1)} convert(f32[2,7168]{1,0:T(2,128)} %layer.1) | non-fusion elementwise | flops 14336 | bytes 86016 | tf_op jit(solution)/shard_map/convert_element_type | solution.py:633

commit v5 on v4

--- a/solution.py
+++ b/solution.py
@@ -62,12 +62,12 @@
 
 
 def layer_kernel(
-    lengths_ref,
+    lengths_hbm,
     queries_ref,
     cache_ref,
     hidden_ref,
-    ids_ref,
-    route_ref,
+    ids_hbm,
+    route_hbm,
     gain_ref,
     value_up_ref,
     out_proj_ref,
@@ -75,6 +75,9 @@
     w_up_ref,
     w_down_ref,
     out_ref,
+    lengths_ref,
+    ids_ref,
+    route_ref,
     query_buf,
     hidden_rows,
     gain_row,
@@ -104,6 +107,7 @@
     rows_all,
     to_axis,
     from_axis,
+    back_axis,
     heads_by_axis,
     units_by_axis,
     weight_by_axis,
@@ -159,22 +163,37 @@
         )
         for index, (source, target) in enumerate(weights)
     ]
-    cache_loads = [
-        pltpu.make_async_copy(cache_ref.at[row], cache_buf.at[row], cache_sem.at[row])
-        for row in range(ROWS_DEV)
-    ]
+    cache_loads = []
+    for row in range(ROWS_DEV):
+        for piece in range(4):
+            depth = pl.ds(piece * 144, 144)
+            cache_loads.append(
+                pltpu.make_async_copy(
+                    cache_ref.at[row, depth, :],
+                    cache_buf.at[row, depth, :],
+                    cache_sem.at[row, piece],
+                )
+            )
     small_loads = [
         pltpu.make_async_copy(source, target, small_sem.at[index])
         for index, (source, target) in enumerate(
-            ((queries_ref, query_buf), (hidden_ref, hidden_rows), (gain_ref, gain_row))
+            (
+                (queries_ref, query_buf),
+                (hidden_ref, hidden_rows),
+                (gain_ref, gain_row),
+                (lengths_hbm, lengths_ref),
+                (ids_hbm, ids_ref),
+                (route_hbm, route_ref),
+            )
         )
     ]
     for copy in [small_loads[0]] + cache_loads + small_loads[1:]:
         copy.start()
     greet_all()
     small_loads[0].wait()
-    cache_loads[0].wait()
-    cache_loads[1].wait()
+    small_loads[3].wait()
+    for load in cache_loads:
+        load.wait()
     for load in loads:
         load.start()
 
@@ -223,15 +242,15 @@
             device_id=(sec, peer),
             device_id_type=MESH,
         ).start()
-    for swap in swaps[2:]:
-        swap.start()
     by_head[me] = msg_buf[me]
 
     rows_i, cols_i = iota(0), iota(1)
     for kind in range(3):
         to_axis[kind] = one_hot(Axis(kind).key(rows_i), cols_i)
-        from_axis[kind] = one_hot(rows_i, Axis(kind).key(cols_i))
-    small_loads[1].wait()
+        from_axis[kind] = one_hot(Axis(0).key(rows_i), Axis(kind).key(cols_i))
+        back_axis[kind] = one_hot(Axis(kind).key(rows_i), Axis(0).key(cols_i))
+    for index in (1, 4, 5):
+        small_loads[index].wait()
     small_loads[2].wait()
     hidden = hidden_rows[...].astype(F32)
     gains = gain_row[...]
@@ -419,6 +438,8 @@
     upper = [jnp.zeros((128, 256), F32) for piece in range(2)]
 
     def common_order(chunk, block):
+        if axes[chunk].kind == 0:
+            return block
         return jnp.dot(
             from_axis[axes[chunk].kind], block, preferred_element_type=F32
         ).astype(BF16)
@@ -441,6 +462,8 @@
 
     each(send_sums, 0)
     each(send_sums, 1)
+    for swap in swaps[2:]:
+        swap.start()
     each(add_sums, 0)
     each(add_sums, 1)
     each(send_rows, 0)
@@ -467,7 +490,7 @@
             value / (1.0 + jnp.exp(-value)) * (factor * upper[piece])
         ).astype(BF16)
     for kind in range(3):
-        hidden_units = jnp.dot(to_axis[kind], rows_all[...], preferred_element_type=F32)
+        hidden_units = jnp.dot(back_axis[kind], rows_all[...], preferred_element_type=F32)
         units_by_axis[kind] = hidden_units[:, 0:512].astype(BF16)
         for piece in range(2):
             expert = piece * 8 + me // 8
@@ -524,16 +547,18 @@
 
 def layer(lengths, queries, cache, hidden_in, expert_ids, route_weights, norm_gain, value_up, out_proj, w_gate, w_up, w_down):
     vmem = pl.BlockSpec(memory_space=pltpu.VMEM)
-    smem = pl.BlockSpec(memory_space=pltpu.SMEM)
     hbm = pl.BlockSpec(memory_space=pl.ANY)
     dma = pltpu.SemaphoreType.DMA
     wides = [tiles * 128 for tiles in TILES]
     return pl.pallas_call(
         layer_kernel,
         out_shape=jax.ShapeDtypeStruct((2, 7168), F32),
-        in_specs=[smem, hbm, hbm, hbm, smem, smem, hbm, hbm, hbm, hbm, hbm, hbm],
+        in_specs=[hbm, hbm, hbm, hbm, hbm, hbm, hbm, hbm, hbm, hbm, hbm, hbm],
         out_specs=vmem,
         scratch_shapes=[
+            pltpu.SMEM((2,), jnp.int32),
+            pltpu.SMEM((2, 8), jnp.int32),
+            pltpu.SMEM((2, 8), F32),
             pltpu.VMEM((2, 576, 128), BF16),
             pltpu.VMEM((2, 7168), BF16),
             pltpu.VMEM((1, 7168), F32),
@@ -563,6 +588,7 @@
             pltpu.VMEM((128, 640), BF16),
             pltpu.VMEM((3, 128, 128), BF16),
             pltpu.VMEM((3, 128, 128), BF16),
+            pltpu.VMEM((3, 128, 128), BF16),
             pltpu.VMEM((3, 128, 256), BF16),
             pltpu.VMEM((3, 128, 512), BF16),
             pltpu.VMEM((3, 2, 128, 128), F32),
@@ -570,8 +596,8 @@
             [pltpu.VMEM((4, 32, wide), BF16) for wide in wides],
             [pltpu.VMEM((16, 2 * sub, 128), BF16) for sub in SUBS],
             [pltpu.VMEM((16, 2 * sub, 128), BF16) for sub in SUBS],
-            dma((3,)),
-            dma((2,)),
+            dma((6,)),
+            dma((2, 4)),
             dma((5,)),
             dma((5,)),
             dma((5,)),

time: 64.3 us -> 63.4 us (0.986)
  Pallas kernels: 62.6 us -> 61.8 us
    pallas_call x1, Pallas kernels: 62.6 us -> 61.8 us  [layer(): pl.pallas_call(layer_kernel, out_shape=jax.ShapeDtypeStruct((2, 7168), F3...]
where the time goes in v5:
time: 63.4 us; the launch traced here: 63.3 us
  Pallas kernels  61.8 us (97%)
  other arithmetic  1.45 us (2%)
    pallas_call x1, Pallas kernels, layer(): pl.pallas_call(layer_kernel, out_shape=jax.ShapeDtypeStruct((2, 7168), F3...  61.8 us
    convert_element_type x1, other arithmetic, per_device(): return out.astype(BF16)  1.45 us

profile of v5, /device:TPU:0, one launch (start us, length us, event | category | flops | bytes accessed | tf_op | source)
XLA Modules:
  0.0 63.3 jit_solution(4448748519485483516)
XLA Ops:
  0.0 61.8 %layer.1 = f32[2,7168]{1,0:T(2,128)} custom-call(s32[2]{0:T(128)} %lengths_hbm.1, bf16[2,576,128]{2,1,0:T(8,128)(2,1)} %bitcast.5, bf16[2,576,2048]{2,1,0:T(8,128)(2,1)} %bitcast.4, bf16[2,7168]{1,0:T(2,128)(2,1)} %hidden_ref.1, s32[2,8]{1,0:T(2,128)} %ids_hbm.1, f32[2,8]{1,0:T(2,128)} %route_hbm.1, f32[1,7168]{1,0:T(1,128)} %bitcast.7, ...), custom_call_target="tpu_custom_call" | custom-call | tf_op jit(solution)/shard_map/layer/pallas_call | solution.py:553
  61.8 1.4 %convert_element_type.3 = bf16[2,7168]{1,0:T(2,128)(2,1)} convert(f32[2,7168]{1,0:T(2,128)} %layer.1) | non-fusion elementwise | flops 14336 | bytes 86016 | tf_op jit(solution)/shard_map/convert_element_type | solution.py:659

commit v6 on v5

--- a/solution.py
+++ b/solution.py
@@ -110,7 +110,6 @@
     back_axis,
     heads_by_axis,
     units_by_axis,
-    weight_by_axis,
     back_out,
     back_in,
     plane_out2,
@@ -194,7 +193,7 @@
     small_loads[3].wait()
     for load in cache_loads:
         load.wait()
-    for load in loads:
+    for load in loads[:2]:
         load.start()
 
     span, step_len = cache_ref.shape[2], 512
@@ -372,8 +371,10 @@
         heads = heads_by_axis[axes[chunk].kind]
         columns = columns_of(chunk)
         product = jnp.dot(
-            heads[:, 0:128], op_buf[0, :, columns], preferred_element_type=F32
-        ) + jnp.dot(heads[:, 128:256], op_buf[1, :, columns], preferred_element_type=F32)
+            heads,
+            op_buf[:, :, columns].reshape(256, TILES[chunk] * 128),
+            preferred_element_type=F32,
+        )
         sums_out[chunk][...] = product.astype(BF16).reshape(sums_out[chunk].shape)
         start_reduce(chunk, sums_out, sums_in, 0)
 
@@ -462,8 +463,8 @@
 
     each(send_sums, 0)
     each(send_sums, 1)
-    for swap in swaps[2:]:
-        swap.start()
+    for copy in loads[2:] + swaps[2:]:
+        copy.start()
     each(add_sums, 0)
     each(add_sums, 1)
     each(send_rows, 0)
@@ -483,34 +484,27 @@
     factor = jnp.sum(
         jnp.where((cols_i >= 48) & (cols_i < 51), named.astype(F32), 0.0), axis=1, keepdims=True
     )
-    rows_all[:, 512:640] = named
     for piece in range(2):
+        expert = piece * 8 + me // 8
+        mine = (cols_i < 48) & (cols_i % EXPERTS == expert)
+        weight = jnp.sum(jnp.where(mine, named.astype(F32), 0.0), axis=1, keepdims=True)
         value = factor * gate[piece]
         rows_all[:, piece * 256 : piece * 256 + 256] = (
-            value / (1.0 + jnp.exp(-value)) * (factor * upper[piece])
+            value / (1.0 + jnp.exp(-value)) * (factor * upper[piece]) * weight
         ).astype(BF16)
-    for kind in range(3):
-        hidden_units = jnp.dot(back_axis[kind], rows_all[...], preferred_element_type=F32)
-        units_by_axis[kind] = hidden_units[:, 0:512].astype(BF16)
-        for piece in range(2):
-            expert = piece * 8 + me // 8
-            mine = (cols_i < 48) & (cols_i % EXPERTS == expert)
-            weight = jnp.sum(
-                jnp.where(mine, hidden_units[:, 512:640], 0.0), axis=1, keepdims=True
-            )
-            weight_by_axis[kind, piece] = jnp.broadcast_to(weight, (128, 128))
+    units_by_axis[0] = rows_all[...]
+    for kind in range(1, 3):
+        units_by_axis[kind] = jnp.dot(
+            back_axis[kind], rows_all[...], preferred_element_type=F32
+        ).astype(BF16)
 
     def send_back(chunk):
-        units = units_by_axis[axes[chunk].kind]
         columns = columns_of(chunk)
-        product = jnp.zeros((128, TILES[chunk] * 128), F32)
-        for piece in range(2):
-            weight = weight_by_axis[axes[chunk].kind, piece]
-            product = product + jnp.concatenate([weight] * TILES[chunk], axis=1) * jnp.dot(
-                units[:, piece * 256 : piece * 256 + 256],
-                wd_buf[piece, :, columns],
-                preferred_element_type=F32,
-            )
+        product = jnp.dot(
+            units_by_axis[axes[chunk].kind],
+            wd_buf[:, :, columns].reshape(512, TILES[chunk] * 128),
+            preferred_element_type=F32,
+        )
         back_out[chunk][...] = product.astype(BF16).reshape(back_out[chunk].shape)
         start_reduce(chunk, back_out, back_in, 2)
 
@@ -585,13 +579,12 @@
             [pltpu.VMEM((16, 2 * sub, 128), BF16) for sub in SUBS],
             [pltpu.VMEM((2 * sub, 128), BF16) for sub in SUBS],
             [pltpu.VMEM((4, 32, wide), BF16) for wide in wides],
-            pltpu.VMEM((128, 640), BF16),
+            pltpu.VMEM((128, 512), BF16),
             pltpu.VMEM((3, 128, 128), BF16),
             pltpu.VMEM((3, 128, 128), BF16),
             pltpu.VMEM((3, 128, 128), BF16),
             pltpu.VMEM((3, 128, 256), BF16),
             pltpu.VMEM((3, 128, 512), BF16),
-            pltpu.VMEM((3, 2, 128, 128), F32),
             [pltpu.VMEM((4, 32, wide), BF16) for wide in wides],
             [pltpu.VMEM((4, 32, wide), BF16) for wide in wides],
             [pltpu.VMEM((16, 2 * sub, 128), BF16) for sub in SUBS],

time: 63.4 us -> 63.1 us (level)
  no operation moved by 1% of the time
where the time goes in v6:
time: 63.1 us; the launch traced here: 62.9 us
  Pallas kernels  61.5 us (97%)
  other arithmetic  1.45 us (2%)
    pallas_call x1, Pallas kernels, layer(): pl.pallas_call(layer_kernel, out_shape=jax.ShapeDtypeStruct((2, 7168), F3...  61.5 us
    convert_element_type x1, other arithmetic, per_device(): return out.astype(BF16)  1.45 us

profile of v6, /device:TPU:0, one launch (start us, length us, event | category | flops | bytes accessed | tf_op | source)
XLA Modules:
  0.0 62.9 jit_solution(4807333083979728427)
XLA Ops:
  0.0 61.5 %layer.1 = f32[2,7168]{1,0:T(2,128)} custom-call(s32[2]{0:T(128)} %lengths_hbm.1, bf16[2,576,128]{2,1,0:T(8,128)(2,1)} %bitcast.5, bf16[2,576,2048]{2,1,0:T(8,128)(2,1)} %bitcast.4, bf16[2,7168]{1,0:T(2,128)(2,1)} %hidden_ref.1, s32[2,8]{1,0:T(2,128)} %ids_hbm.1, f32[2,8]{1,0:T(2,128)} %route_hbm.1, f32[1,7168]{1,0:T(1,128)} %bitcast.7, ...), custom_call_target="tpu_custom_call" | custom-call | tf_op jit(solution)/shard_map/layer/pallas_call | solution.py:547
  61.5 1.4 %convert_element_type.3 = bf16[2,7168]{1,0:T(2,128)(2,1)} convert(f32[2,7168]{1,0:T(2,128)} %layer.1) | non-fusion elementwise | flops 14336 | bytes 86016 | tf_op jit(solution)/shard_map/convert_element_type | solution.py:652
